TPU v7x, 128 devices: a whole 4x4x4 slice. The times are simulated.
128 devices in a mesh: exp: 32 (over z, x, core), rep: 4 (over y).
Axes of the slice: x: 4, y: 4, z: 4, core: 2. Of those that a mesh axis runs over, the one named last changes fastest.
Arguments:
- images: bfloat16 [256, 256, 1024], P(('exp', 'rep')), may hold values from -12 to 12
- router: float32 [1024, 128], P(('exp', 'rep')), may hold values from -4 to 4
- w_in: bfloat16 [128, 1024, 2560], P(('exp', 'rep')), may hold values from -0.1875 to 0.1875
- w_out: bfloat16 [128, 2560, 1024], P(('exp', 'rep')), may hold values from -0.125 to 0.125
- out_grad: bfloat16 [256, 256, 1024], P(('exp', 'rep')), may hold values from -6 to 6
Outputs:
- images_grad: bfloat16 [256, 256, 1024], P(('exp', 'rep'))
- w_in_grad: bfloat16 [128, 1024, 2560], P(('exp', 'rep'))
- w_out_grad: bfloat16 [128, 2560, 1024], P(('exp', 'rep'))
- router_grad: float32 [1024, 128], P(('exp', 'rep'))
All inputs are finite; a program needn't handle non-finite values.
Results may differ from a plain program's by a relative error of at most 0.012.
The roundings to bfloat16 on the way count: a program that leaves them out, or rounds other values in their place, can miss the bound.
Values may be sent and summed in bfloat16 or wider, within the bound.
No kernel may reach another device: no remote copies, remote signals or barrier semaphores. Data moves between devices by JAX's collectives and lax.ppermute only.
A program may use at most 128 MiB of HBM per device.

v0:
```python
import jax
import jax.numpy as jnp
from jax import lax
from jax.sharding import PartitionSpec as P

LOGIT_SCALE = 2.0
EPS = 1e-06
SQRT_HALF = 0.7071067811865476
INV_ROOT = 0.3989422804014327


def gelu_parts(pre_value):
    cumulative = 0.5 * (1.0 + lax.erf(pre_value * SQRT_HALF))
    gelu_slope = cumulative + pre_value * jnp.exp(-0.5 * pre_value * pre_value) * INV_ROOT
    return (pre_value * cumulative, gelu_slope)


def contract_last(left_side, right_side):
    return lax.dot_general(
        left_side, right_side, (((1,), (1,)), ((), ())), preferred_element_type=jnp.float32
    )


def contract_first(left_side, right_side):
    return lax.dot_general(
        left_side, right_side, (((0,), (0,)), ((), ())), preferred_element_type=jnp.float32
    )


def expert_pass(slot_rows, slot_grads, weight_in, weight_out):
    pre_act = jnp.dot(slot_rows, weight_in, preferred_element_type=jnp.float32)
    activated, gelu_slope = gelu_parts(pre_act)
    hidden = activated.astype(jnp.bfloat16)
    slot_out = jnp.dot(hidden, weight_out, preferred_element_type=jnp.float32).astype(jnp.bfloat16)
    hidden_grad = contract_last(slot_grads, weight_out)
    pre_grad = (hidden_grad * gelu_slope).astype(jnp.bfloat16)
    grad_out = contract_first(hidden, slot_grads).astype(jnp.bfloat16)
    grad_in = contract_first(slot_rows, pre_grad).astype(jnp.bfloat16)
    slot_dx = contract_last(pre_grad, weight_in).astype(jnp.bfloat16)
    return (slot_out, slot_dx, grad_in, grad_out)


def per_device(images, router, w_in, w_out, out_grad):
    model_width = images.shape[2]
    router_whole = lax.all_gather(router, ("exp", "rep"), axis=0, tiled=True)
    inv_norm = lax.rsqrt(jnp.sum(router_whole * router_whole, axis=0) + EPS)
    router_low = (router_whole * inv_norm).astype(jnp.bfloat16)
    logits = LOGIT_SCALE * jnp.einsum(
        "btd,de->bte", images, router_low, preferred_element_type=jnp.float32
    )
    dispatch = jax.nn.softmax(logits, axis=1)
    combine = jax.nn.softmax(logits, axis=2)
    dispatch_low = dispatch.astype(jnp.bfloat16)
    combine_low = combine.astype(jnp.bfloat16)
    slot_in = jnp.einsum(
        "bte,btd->bed", dispatch_low, images, preferred_element_type=jnp.float32
    ).astype(jnp.bfloat16)
    slot_grad = jnp.einsum(
        "bte,btd->bed", combine_low, out_grad, preferred_element_type=jnp.float32
    ).astype(jnp.bfloat16)
    paired = jnp.stack((slot_in, slot_grad), axis=0)
    arrived = lax.all_to_all(paired, ("exp", "rep"), split_axis=2, concat_axis=1, tiled=True)
    arrived = arrived.reshape(2, -1, model_width)
    slot_out, slot_dx, grad_in, grad_out = expert_pass(arrived[0], arrived[1], w_in[0], w_out[0])
    results = jnp.stack((slot_out, slot_dx), axis=0)
    returned = lax.all_to_all(
        results[:, :, None, :], ("exp", "rep"), split_axis=1, concat_axis=2, tiled=True
    )
    combine_grad = jnp.einsum(
        "btd,bed->bte", out_grad, returned[0], preferred_element_type=jnp.float32
    )
    grad_combine = combine * (combine_grad - jnp.sum(combine * combine_grad, axis=2, keepdims=True))
    dispatch_grad = jnp.einsum(
        "btd,bed->bte", images, returned[1], preferred_element_type=jnp.float32
    )
    grad_dispatch = dispatch * (
        dispatch_grad - jnp.sum(dispatch * dispatch_grad, axis=1, keepdims=True)
    )
    logit_grad = (LOGIT_SCALE * (grad_combine + grad_dispatch)).astype(jnp.bfloat16)
    images_grad = (
        jnp.einsum("bte,bed->btd", dispatch_low, returned[1], preferred_element_type=jnp.float32)
        + jnp.einsum("bte,de->btd", logit_grad, router_low, preferred_element_type=jnp.float32)
    ).astype(jnp.bfloat16)
    hat_rows = lax.psum_scatter(
        jnp.einsum("btd,bte->de", images, logit_grad, preferred_element_type=jnp.float32),
        ("exp", "rep"),
        scatter_dimension=0,
        tiled=True,
    )
    own_hat = router * inv_norm
    own_low = lax.optimization_barrier(own_hat.astype(jnp.bfloat16)).astype(jnp.float32)
    moment = lax.psum(jnp.sum(own_low * hat_rows, axis=0), ("exp", "rep"))
    router_grad = (hat_rows - own_hat * moment) * inv_norm
    return (images_grad, grad_in[None], grad_out[None], router_grad)


def solution(mesh):
    in_specs = (
        P(("exp", "rep"), None, None),
        P(("exp", "rep"), None),
        P(("exp", "rep"), None, None),
        P(("exp", "rep"), None, None),
        P(("exp", "rep"), None, None),
    )
    out_specs = (
        P(("exp", "rep"), None, None),
        P(("exp", "rep"), None, None),
        P(("exp", "rep"), None, None),
        P(("exp", "rep"), None),
    )
    return jax.shard_map(
        per_device, mesh=mesh, in_specs=in_specs, out_specs=out_specs, check_vma=False
    )
```

profile of v0, /device:TPU:1, one launch (start us, length us, event | category | flops | bytes accessed | tf_op | source)
XLA Modules:
  0.0 350.7 jit_solution(596781061575463216)
XLA Ops:
  7.2 0.0 copy-start
  7.2 54.5 %all_gather.3 = f32[1024,128]{1,0:T(8,128)S(1)} all-gather(f32[8,128]{1,0:T(8,128)} %param.6), channel_id=1, replica_groups=mesh['exp'=32,'rep'=4] {'exp','rep'}, dimensions={0}, use_global_device_ids=true | all-gather | bytes 528384 | tf_op jit(solution)/shard_map/all_gather | solution.py:45
  61.7 0.1 multiply_reduce_fusion
  61.9 0.7 copy-done.1
  62.5 0.0 copy-done
  62.5 0.5 fusion.48
  63.0 0.0 copy-start.5
  63.0 0.8 fusion.70
  63.8 0.8 fusion.69
  64.6 0.6 fusion.30
  65.2 0.0 copy-done.9
  65.2 0.3 fusion.31
  65.5 0.1 pad_maximum_fusion
  65.6 0.0 copy-done.5
  65.6 1.1 copy.51
  66.7 25.0 %all_to_all.30 = bf16[2,2,128,1024]{3,1,0,2:T(2,128)(2,1)S(1)} all-to-all(bf16[2,2,128,1024]{3,1,0,2:T(2,128)(2,1)S(1)} %copy.51), channel_id=1, replica_groups=mesh['exp'=32,'rep'=4] {'exp','rep'}, dimensions={2} | all-to-all | bytes 2097152 | tf_op jit(solution)/shard_map/all_to_all | solution.py:62
  91.8 0.7 fusion.68
  92.5 0.2 squeeze.19
  92.7 0.0 copy-start.3
  92.7 0.2 squeeze.22
  92.9 0.0 copy-start.6
  92.9 0.0 slice-start
  92.9 0.0 slice-start.2
  92.9 3.8 %multiply_convert_fusion = (bf16[256,2560]{1,0:T(8,128)(2,1)S(1)}, f32[256,2560]{1,0:T(8,128)S(1)}) fusion(bf16[256,1024]{1,0:T(8,128)(2,1)S(1)} %squeeze.19, bf16[1,1024,2560]{2,1,0:T(8,128)(2,1)} %param.7), kind=kOutput, calls=%fused_computation.23 | convolution fusion | flops 1345454080 | bytes 9699328 | tf_op jit(solution)/shard_map/dot_general | solution.py:31
  96.7 0.0 copy-done.3
  96.7 0.0 copy-done.6
  96.8 0.0 slice-start.1
  96.8 0.0 slice-start.3
  96.8 5.1 %fusion.17 = bf16[256,2560]{1,0:T(8,128)(2,1)S(1)} fusion(bf16[256,1024]{1,0:T(8,128)(2,1)S(1)} %squeeze.22, bf16[1,2560,1024]{2,1,0:T(8,128)(2,1)} %param.8, f32[256,2560]{1,0:T(8,128)S(1)} %get-tuple-element.27), kind=kOutput, calls=%fused_computation.18 | convolution fusion | flops 1348730880 | bytes 9699328 | tf_op jit(solution)/shard_map/dot_general | solution.py:19
  101.8 0.0 slice-done
  101.9 0.0 slice-done.1
  101.9 0.0 copy-start.7
  101.9 1.5 fusion.35
  103.4 0.0 copy-done.7
  103.5 0.0 slice-done.2
  103.5 0.0 slice-done.3
  103.5 1.5 fusion.32
  105.0 0.1 maximum_bitcast_fusion
  105.1 0.0 copy-start.13
  105.1 2.0 copy.52
  107.2 4.0 %all-to-all-start.1 = ((bf16[2,256,1,1024]{3,0,2,1:T(2,128)(2,1)}), bf16[2,256,1,1024]{3,0,2,1:T(2,128)(2,1)S(1)}, u32[]{:S(2)}, u32[]{:S(2)}) async-start(bf16[2,256,1,1024]{3,0,2,1:T(2,128)(2,1)} %copy.52), calls=%async_computation.1 | async-start | bytes 2097152 | tf_op jit(solution)/shard_map/all_to_all | solution.py:66
  111.2 0.0 all-reduce.3.cloned.1.call-start
  111.2 0.0 copy-done.13
  111.3 0.0 copy-start.4
  111.3 0.0 copy-start.8
  111.3 5.1 %fusion.13 = bf16[1,2560,1024]{2,1,0:T(8,128)(2,1)} fusion(bf16[256,2560]{1,0:T(8,128)(2,1)S(1)} %get-tuple-element.26, bf16[256,1024]{1,0:T(8,128)(2,1)} %copy-done.6), kind=kOutput, calls=%fused_computation.15 | convolution fusion | flops 1344798720 | bytes 7077888 | tf_op jit(solution)/shard_map/dot_general | solution.py:25
  116.4 0.0 copy-done.4
  116.4 0.0 copy-done.8
  116.4 3.9 %fusion.12 = bf16[1,1024,2560]{2,1,0:T(8,128)(2,1)} fusion(bf16[256,1024]{1,0:T(8,128)(2,1)S(1)} %copy-done.4, bf16[256,2560]{1,0:T(8,128)(2,1)S(1)} %copy-done.8), kind=kOutput, calls=%fused_computation.14 | convolution fusion | flops 1344798720 | bytes 7077888 | tf_op jit(solution)/shard_map/dot_general | solution.py:25
  120.3 10.4 %all-to-all-done.1 = bf16[2,256,1,1024]{3,0,2,1:T(2,128)(2,1)S(1)} async-done(((bf16[2,256,1,1024]{3,0,2,1:T(2,128)(2,1)}), bf16[2,256,1,1024]{3,0,2,1:T(2,128)(2,1)S(1)}, u32[]{:S(2)}, u32[]{:S(2)}) %all-to-all-start.1) | async-done | bytes 1048608 | tf_op jit(solution)/shard_map/all_to_all | solution.py:66
  130.7 0.3 copy.65
  131.1 0.5 convolution_bitcast_fusion.2
  131.6 0.5 convolution_bitcast_fusion.1
  132.1 1.1 fusion.44
  133.2 0.0 copy-start.12
  133.2 2.3 convolution_bitcast_fusion
  135.5 1.8 fusion.50
  137.3 0.0 all-reduce.3.cloned.1.call-update
  137.4 2.9 add_convert_fusion
  140.2 138.1 %all-reduce.3.cloned.1.call-done = f32[1024,128]{0,1:T(8,128)} async-done(((f32[1024,128]{0,1:T(8,128)}), f32[1024,128]{0,1:T(8,128)}) %all-reduce.3.cloned.1.call-update) | async-done | bytes 524304
  278.3 0.9 constant_dynamic-slice_fusion
  279.3 0.1 copy.57
  279.3 63.9 %psum.7 = f32[128]{0:T(128)S(1)} all-reduce(f32[128]{0:T(128)S(1)} %multiply_reduce_fusion.3), channel_id=1, replica_groups=mesh['exp'=32,'rep'=4] {'exp','rep'}, use_global_device_ids=true, to_apply=%region_9.0 | all-reduce | flops 128 | bytes 1024 | tf_op jit(solution)/shard_map/psum | solution.py:92
  343.2 0.6 subtract_multiply_fusion
  (14 shorter events, 0.1 us)
Async XLA Ops:
  7.2 55.4 %copy-start = (bf16[2,256,1024]{2,1,0:T(8,128)(2,1)S(1)}, bf16[2,256,1024]{2,1,0:T(8,128)(2,1)}, u32[]{:S(2)}) copy-start(bf16[2,256,1024]{2,1,0:T(8,128)(2,1)} %param.5) | copy-start | bytes 3145732
  61.7 0.8 copy-start.1
  61.7 3.5 copy-start.9
  63.0 2.6 copy-start.5
  92.7 4.0 %copy-start.3 = (bf16[256,1024]{1,0:T(8,128)(2,1)}, bf16[256,1024]{1,0:T(8,128)(2,1)S(1)}, u32[]{:S(2)}) copy-start(bf16[256,1024]{1,0:T(8,128)(2,1)S(1)} %squeeze.19) | copy-start | bytes 1572868
  92.9 3.8 %copy-start.6 = (bf16[256,1024]{1,0:T(8,128)(2,1)}, bf16[256,1024]{1,0:T(8,128)(2,1)S(1)}, u32[]{:S(2)}) copy-start(bf16[256,1024]{1,0:T(8,128)(2,1)S(1)} %squeeze.22) | copy-start | bytes 1572868
  92.9 8.9 %slice-start = ((s8[5242880]{0:T(1024)(128)(4,1)}), s8[4194304]{0:T(1024)(128)(4,1)S(1)}, s32[]{:S(2)}) async-start(s8[5242880]{0:T(1024)(128)(4,1)} %bitcast.97), calls=%async_computation.3 | async-start | bytes 8388608
  92.9 10.5 %slice-start.2 = ((s8[5242880]{0:T(1024)(128)(4,1)}), s8[4194304]{0:T(1024)(128)(4,1)S(1)}, s32[]{:S(2)}) async-start(s8[5242880]{0:T(1024)(128)(4,1)} %bitcast.99), calls=%async_computation.5 | async-start | bytes 8388608
  96.8 5.1 %slice-start.1 = ((s8[5242880]{0:T(1024)(128)(4,1)}), s8[1048576]{0:T(1024)(128)(4,1)S(1)}, s32[]{:S(2)}) async-start(s8[5242880]{0:T(1024)(128)(4,1)} %bitcast.97), calls=%async_computation.4 | async-start | bytes 2097152
  96.8 6.7 %slice-start.3 = ((s8[5242880]{0:T(1024)(128)(4,1)}), s8[1048576]{0:T(1024)(128)(4,1)S(1)}, s32[]{:S(2)}) async-start(s8[5242880]{0:T(1024)(128)(4,1)} %bitcast.99), calls=%async_computation.6 | async-start | bytes 2097152
  101.9 1.6 copy-start.7
  105.1 6.1 %copy-start.13 = (f32[8,128]{1,0:T(8,128)S(1)}, f32[8,128]{1,0:T(8,128)}, u32[]{:S(2)}) copy-start(f32[8,128]{1,0:T(8,128)} %param.6) | copy-start | bytes 12292
  107.2 23.6 %all-to-all-start.1 = ((bf16[2,256,1,1024]{3,0,2,1:T(2,128)(2,1)}), bf16[2,256,1,1024]{3,0,2,1:T(2,128)(2,1)S(1)}, u32[]{:S(2)}, u32[]{:S(2)}) async-start(bf16[2,256,1,1024]{3,0,2,1:T(2,128)(2,1)} %copy.52), calls=%async_computation.1 | async-start | bytes 2097152 | tf_op jit(solution)/shard_map/all_to_all | solution.py:66
  111.2 167.2 %all-reduce.3.cloned.1.call-start = ((), (), s32[]{:S(2)}) async-start(), calls=%async_computation.2 | async-start | bytes 1048576
  111.3 5.1 %copy-start.4 = (bf16[256,1024]{1,0:T(8,128)(2,1)S(1)}, bf16[256,1024]{1,0:T(8,128)(2,1)}, u32[]{:S(2)}) copy-start(bf16[256,1024]{1,0:T(8,128)(2,1)} %copy-done.3) | copy-start | bytes 1572868
  111.3 5.1 %copy-start.8 = (bf16[256,2560]{1,0:T(8,128)(2,1)S(1)}, bf16[256,2560]{1,0:T(8,128)(2,1)}, u32[]{:S(2)}) copy-start(bf16[256,2560]{1,0:T(8,128)(2,1)} %copy-done.7) | copy-start | bytes 3932164
  116.4 14.7 %copy-start.10 = (bf16[2,256,1024]{2,1,0:T(8,128)(2,1)S(1)}, bf16[2,256,1024]{2,1,0:T(8,128)(2,1)}, u32[]{:S(2)}) copy-start(bf16[2,256,1024]{2,1,0:T(8,128)(2,1)} %param.9) | copy-start | bytes 3145732
  130.7 1.3 copy-start.11
  131.1 2.1 copy-start.2
  133.2 2.3 copy-start.12
Sparse Core Ops, SparseCore 0:
  137.5 140.8 all-reduce.2
where the time goes:
time: 351 us
  waiting for transfers between devices  149 us (42%)
  blocking collectives  143 us (41%)
  matrix products  30.2 us (9%)
  between operations  14.4 us (4%)
  local copies, waits for them, and re-layouts  6.28 us (2%)
  starting transfers between devices  4.04 us (1%)
  other arithmetic  3.69 us (1%)
    unnamed x2, waiting for transfers between devices  138 us
    psum x1, blocking collectives, per_device(): moment = lax.psum(jnp.sum(own_low * hat_rows, axis=0), ('exp', 'rep'))  63.9 us
    all_gather x1, blocking collectives, per_device(): router_whole = lax.all_gather(router, ('exp', 'rep'), axis=0, tiled=True)  54.5 us
    all_to_all x1, blocking collectives, per_device(): lax.all_to_all(paired, ('exp', 'rep'), split_axis=2, concat_axis=1, tiled...  25 us
    all_to_all x1, waiting for transfers between devices, per_device(): lax.all_to_all(results[:, :, None, :], ('exp', 'rep'), split_axis=1, conc...  10.4 us
    dot_general x2, matrix products, contract_first(): lax.dot_general(left_side, right_side, (((0,), (0,)), ((), ())), preferre...  9.01 us
  transfers between devices with their start and end apart: 2, of which 2 were waited for; matrix products, arithmetic and copies ran while one was open for 3% of the time, Pallas kernels for 0%

commit v1 on v0

--- a/solution.py
+++ b/solution.py
@@ -5,6 +5,7 @@
 
 LOGIT_SCALE = 2.0
 EPS = 1e-06
+AXES = ("exp", "rep")
 SQRT_HALF = 0.7071067811865476
 INV_ROOT = 0.3989422804014327
 
@@ -40,9 +41,16 @@
     return (slot_out, slot_dx, grad_in, grad_out)
 
 
+def spread_rows(rows):
+    devices = lax.axis_size(AXES)
+    copies = jnp.broadcast_to(rows[None], (devices,) + rows.shape)
+    gathered = lax.all_to_all(copies, AXES, split_axis=0, concat_axis=0, tiled=True)
+    return gathered.reshape(-1, rows.shape[1])
+
+
 def per_device(images, router, w_in, w_out, out_grad):
     model_width = images.shape[2]
-    router_whole = lax.all_gather(router, ("exp", "rep"), axis=0, tiled=True)
+    router_whole = spread_rows(router)
     inv_norm = lax.rsqrt(jnp.sum(router_whole * router_whole, axis=0) + EPS)
     router_low = (router_whole * inv_norm).astype(jnp.bfloat16)
     logits = LOGIT_SCALE * jnp.einsum(
@@ -81,15 +89,18 @@
         jnp.einsum("bte,bed->btd", dispatch_low, returned[1], preferred_element_type=jnp.float32)
         + jnp.einsum("bte,de->btd", logit_grad, router_low, preferred_element_type=jnp.float32)
     ).astype(jnp.bfloat16)
-    hat_rows = lax.psum_scatter(
-        jnp.einsum("btd,bte->de", images, logit_grad, preferred_element_type=jnp.float32),
-        ("exp", "rep"),
-        scatter_dimension=0,
-        tiled=True,
-    )
+    hat_part = jnp.einsum("btd,bte->de", images, logit_grad, preferred_element_type=jnp.float32)
+    low_wide = lax.optimization_barrier(router_low).astype(jnp.float32)
+    moment_part = jnp.sum(low_wide * hat_part, axis=0)
+    devices = lax.axis_size(AXES)
+    blocks = hat_part.reshape(devices, -1, hat_part.shape[1])
+    own_rows = blocks.shape[1]
+    moment_rows = jnp.broadcast_to(moment_part[None, None], (devices, 1, hat_part.shape[1]))
+    sent = jnp.concatenate((blocks, moment_rows), axis=1)
+    terms = lax.all_to_all(sent, AXES, split_axis=0, concat_axis=0, tiled=True)
+    summed = jnp.sum(terms, axis=0)
+    hat_rows, moment = summed[:own_rows], summed[own_rows]
     own_hat = router * inv_norm
-    own_low = lax.optimization_barrier(own_hat.astype(jnp.bfloat16)).astype(jnp.float32)
-    moment = lax.psum(jnp.sum(own_low * hat_rows, axis=0), ("exp", "rep"))
     router_grad = (hat_rows - own_hat * moment) * inv_norm
     return (images_grad, grad_in[None], grad_out[None], router_grad)
 

time: 351 us -> 126 us (0.36)
  waiting for transfers between devices: 149 us -> 25.1 us
  blocking collectives: 143 us -> 48.2 us
  between operations: 14.4 us -> 1.11 us
  starting transfers between devices: 4.04 us -> 8.87 us
    unnamed x2 -> x0, waiting for transfers between devices: 138 us -> none
    psum x1 -> x0, blocking collectives: 63.9 us -> none  [per_device(): moment = lax.psum(jnp.sum(own_low * hat_rows, axis=0), ('exp', 'rep'))]
    all_gather x1 -> x0, blocking collectives: 54.5 us -> none  [per_device(): router_whole = lax.all_gather(router, ('exp', 'rep'), axis=0, tiled=True)]
    all_to_all x0 -> x1, blocking collectives: none -> 25.1 us  [spread_rows(): lax.all_to_all(copies, AXES, split_axis=0, concat_axis=0, tiled=True)]
    all_to_all x0 -> x1, waiting for transfers between devices: none -> 14.5 us  [per_device(): terms = lax.all_to_all(sent, AXES, split_axis=0, concat_axis=0, tiled=True)]
    all_to_all x0 -> x1, starting transfers between devices: none -> 4.87 us  [per_device(): terms = lax.all_to_all(sent, AXES, split_axis=0, concat_axis=0, tiled=True)]
  transfers between devices with their start and end apart: 2 -> 2, of which waited for: 2 -> 2; matrix products, arithmetic and copies ran while one was open for 3% -> 11% of each run, Pallas kernels for 0% -> 0%
where the time goes in v1:
time: 126 us
  blocking collectives  48.2 us (38%)
  matrix products  29.5 us (23%)
  waiting for transfers between devices  25.1 us (20%)
  starting transfers between devices  8.87 us (7%)
  local copies, waits for them, and re-layouts  6.62 us (5%)
  other arithmetic  6.21 us (5%)
    all_to_all x1, blocking collectives, spread_rows(): lax.all_to_all(copies, AXES, split_axis=0, concat_axis=0, tiled=True)  25.1 us
    all_to_all x1, blocking collectives, per_device(): lax.all_to_all(paired, ('exp', 'rep'), split_axis=2, concat_axis=1, tiled...  23.1 us
    all_to_all x1, waiting for transfers between devices, per_device(): terms = lax.all_to_all(sent, AXES, split_axis=0, concat_axis=0, tiled=True)  14.5 us
    all_to_all x1, waiting for transfers between devices, per_device(): lax.all_to_all(results[:, :, None, :], ('exp', 'rep'), split_axis=1, conc...  10.5 us
    dot_general x2, matrix products, contract_first(): lax.dot_general(left_side, right_side, (((0,), (0,)), ((), ())), preferre...  9.01 us
    dot_general x2, matrix products, contract_last(): lax.dot_general(left_side, right_side, (((1,), (1,)), ((), ())), preferre...  6.61 us
    all_to_all x1, starting transfers between devices, per_device(): terms = lax.all_to_all(sent, AXES, split_axis=0, concat_axis=0, tiled=True)  4.87 us
    all_to_all x1, starting transfers between devices, per_device(): lax.all_to_all(results[:, :, None, :], ('exp', 'rep'), split_axis=1, conc...  4 us
  transfers between devices with their start and end apart: 2, of which 2 were waited for; matrix products, arithmetic and copies ran while one was open for 11% of the time, Pallas kernels for 0%

profile of v1, /device:TPU:1, one launch (start us, length us, event | category | flops | bytes accessed | tf_op | source)
XLA Modules:
  0.0 125.5 jit_solution(8431149162212262795)
XLA Ops:
  0.6 0.0 copy-start
  0.6 0.8 broadcast_in_dim.10
  1.5 25.1 %all_to_all.40 = f32[128,8,128]{2,1,0:T(8,128)S(1)} all-to-all(f32[128,8,128]{2,1,0:T(8,128)S(1)} %broadcast_in_dim.10), channel_id=1, replica_groups=mesh['exp'=32,'rep'=4] {'exp','rep'}, dimensions={0} | all-to-all | bytes 1048576 | tf_op jit(solution)/shard_map/all_to_all | solution.py:47
  26.5 0.1 multiply_reduce_fusion.1
  26.7 0.2 copy.29
  26.9 0.0 copy-start.10
  26.9 0.1 multiply_convert_fusion.1
  27.0 0.0 copy-start.5
  27.0 0.7 copy-done.5
  27.7 0.0 copy-done
  27.7 0.5 fusion.48
  28.2 0.0 copy-start.4
  28.2 0.8 fusion.70
  29.1 0.8 fusion.69
  29.8 0.5 fusion.30
  30.4 0.0 copy-done.10
  30.4 0.3 fusion.31
  30.8 0.1 pad_maximum_fusion
  30.9 0.0 copy-done.4
  30.9 1.1 copy.30
  32.0 23.1 %all_to_all.41 = bf16[2,2,128,1024]{3,1,0,2:T(2,128)(2,1)S(1)} all-to-all(bf16[2,2,128,1024]{3,1,0,2:T(2,128)(2,1)S(1)} %copy.30), channel_id=1, replica_groups=mesh['exp'=32,'rep'=4] {'exp','rep'}, dimensions={2} | all-to-all | bytes 2097152 | tf_op jit(solution)/shard_map/all_to_all | solution.py:70
  55.1 0.7 fusion.68
  55.8 0.2 squeeze.19
  56.0 0.0 copy-start.2
  56.0 0.2 squeeze.22
  56.2 0.0 copy-start.7
  56.2 0.0 slice-start
  56.3 0.0 slice-start.2
  56.3 3.8 %multiply_convert_fusion = (bf16[256,2560]{1,0:T(8,128)(2,1)S(1)}, f32[256,2560]{1,0:T(8,128)S(1)}) fusion(bf16[256,1024]{1,0:T(8,128)(2,1)S(1)} %squeeze.19, bf16[1,1024,2560]{2,1,0:T(8,128)(2,1)} %param.7), kind=kOutput, calls=%fused_computation.23 | convolution fusion | flops 1345454080 | bytes 9699328 | tf_op jit(solution)/shard_map/dot_general | solution.py:32
  60.1 0.0 copy-done.2
  60.1 0.0 copy-done.7
  60.1 0.0 slice-start.1
  60.1 0.0 slice-start.3
  60.1 5.1 %fusion.17 = bf16[256,2560]{1,0:T(8,128)(2,1)S(1)} fusion(bf16[256,1024]{1,0:T(8,128)(2,1)S(1)} %squeeze.22, bf16[1,2560,1024]{2,1,0:T(8,128)(2,1)} %param.8, f32[256,2560]{1,0:T(8,128)S(1)} %get-tuple-element.11), kind=kOutput, calls=%fused_computation.18 | convolution fusion | flops 1348730880 | bytes 9699328 | tf_op jit(solution)/shard_map/dot_general | solution.py:20
  65.2 0.0 slice-done
  65.2 0.0 slice-done.1
  65.2 0.0 copy-start.8
  65.2 1.5 %fusion.35 = bf16[1,256,1024]{2,1,0:T(8,128)(2,1)S(1)} fusion(bf16[256,2560]{1,0:T(8,128)(2,1)S(1)} %fusion.17, bf16[1,1024,2560]{2,1,0:T(8,128)(2,1)S(1)} %bitcast.103), kind=kOutput, calls=%fused_computation.33 | convolution fusion | flops 1342439424 | bytes 7077888 | tf_op jit(solution)/shard_map/dot_general | solution.py:20
  66.8 1.5 %fusion.32 = bf16[1,256,1024]{2,1,0:T(8,128)(2,1)S(1)} fusion(bf16[256,2560]{1,0:T(8,128)(2,1)S(1)} %get-tuple-element.10, bf16[1,2560,1024]{2,1,0:T(8,128)(2,1)S(1)} %bitcast.105), kind=kOutput, calls=%fused_computation.32 | convolution fusion | flops 1342439424 | bytes 7077888 | tf_op jit(solution)/shard_map/dot_general | solution.py:35
  68.3 0.1 maximum_bitcast_fusion
  68.4 2.0 %copy.31 = bf16[2,256,1,1024]{3,0,2,1:T(2,128)(2,1)} copy(bf16[2,256,1,1024]{3,1,0,2:T(8,128)(2,1)S(1)} %maximum_bitcast_fusion) | data formatting | bytes 2097152 | tf_op jit(solution)/shard_map/broadcast_in_dim | solution.py:75
  70.5 4.0 %all-to-all-start.2 = ((bf16[2,256,1,1024]{3,0,2,1:T(2,128)(2,1)}), bf16[2,256,1,1024]{3,0,2,1:T(2,128)(2,1)S(1)}, u32[]{:S(2)}, u32[]{:S(2)}) async-start(bf16[2,256,1,1024]{3,0,2,1:T(2,128)(2,1)} %copy.31), calls=%async_computation.2 | async-start | bytes 2097152 | tf_op jit(solution)/shard_map/all_to_all | solution.py:74
  74.5 0.0 copy-start.9
  74.5 5.1 %fusion.13 = bf16[1,2560,1024]{2,1,0:T(8,128)(2,1)} fusion(bf16[256,2560]{1,0:T(8,128)(2,1)S(1)} %get-tuple-element.10, bf16[256,1024]{1,0:T(8,128)(2,1)} %copy-done.7), kind=kOutput, calls=%fused_computation.15 | convolution fusion | flops 1344798720 | bytes 7077888 | tf_op jit(solution)/shard_map/dot_general | solution.py:26
  79.6 0.0 copy-done.9
  79.6 3.9 %fusion.12 = bf16[1,1024,2560]{2,1,0:T(8,128)(2,1)} fusion(bf16[256,1024]{1,0:T(8,128)(2,1)S(1)} %copy-done.3, bf16[256,2560]{1,0:T(8,128)(2,1)S(1)} %copy-done.9), kind=kOutput, calls=%fused_computation.14 | convolution fusion | flops 1344798720 | bytes 7077888 | tf_op jit(solution)/shard_map/dot_general | solution.py:26
  83.5 10.5 %all-to-all-done.2 = bf16[2,256,1,1024]{3,0,2,1:T(2,128)(2,1)S(1)} async-done(((bf16[2,256,1,1024]{3,0,2,1:T(2,128)(2,1)}), bf16[2,256,1,1024]{3,0,2,1:T(2,128)(2,1)S(1)}, u32[]{:S(2)}, u32[]{:S(2)}) %all-to-all-start.2) | async-done | bytes 1048608 | tf_op jit(solution)/shard_map/all_to_all | solution.py:74
  94.1 0.3 copy.42
  94.4 0.5 convolution_bitcast_fusion.2
  94.9 0.0 copy-start.12
  94.9 0.5 convolution_bitcast_fusion.1
  95.4 1.1 fusion.44
  96.6 0.0 copy-start.13
  96.6 0.0 copy-done.6
  96.6 1.6 %multiply_reduce_fusion = (f32[128]{0:T(128)S(1)}, f32[1024,128]{0,1:T(8,128)S(1)}) fusion(bf16[1024,128]{0,1:T(8,128)(2,1)S(1)} %copy-done.6, bf16[2,256,1024]{2,1,0:T(8,128)(2,1)S(1)} %copy-done, f32[2,256,128]{1,2,0:T(8,128)S(1)} %fusion.44, f32[2,256,128]{1,2,0:T(8,128)S(1)} %convolution_bitcast_fusion.2, f32[2,256,128]{1,2,0:T(8,128)} %get-tuple-element.7, ...), kind=kOutput, calls=%fused_computation.57 | convolution fusion | flops 135135744 | bytes 2624000 | tf_op jit(solution)/shard_map/btd,bte->de/dot_general | solution.py:92
  98.2 0.2 copy.36
  98.4 1.1 pad_maximum_fusion.1
  99.5 4.9 %all-to-all-start.3 = ((f32[128,9,128]{2,1,0:T(8,128)}), f32[128,9,128]{2,1,0:T(8,128)}, u32[]{:S(2)}, u32[]{:S(2)}) async-start(f32[128,9,128]{2,1,0:T(8,128)} %pad_maximum_fusion.1), calls=%async_computation.3 | async-start | bytes 2097152 | tf_op jit(solution)/shard_map/all_to_all | solution.py:100
  104.3 1.8 %fusion.50 = f32[2,256,1024]{2,1,0:T(8,128)S(1)} fusion(f32[2,256,128]{1,2,0:T(8,128)} %copy-done.13, f32[2,256,128]{1,2,0:T(8,128)} %copy-done.12, bf16[1024,128]{0,1:T(8,128)(2,1)S(1)} %copy-done.6, f32[2,256,128]{1,2,0:T(8,128)} %get-tuple-element.7, f32[2,256]{1,0:T(2,128)S(1)} %get-tuple-element.6), kind=kOutput, calls=%fused_computation.54 | convolution fusion | flops 134742656 | bytes 3147776 | tf_op jit(solution)/shard_map/bte,de->btd/dot_general | solution.py:90
  106.1 0.0 copy-start.15
  106.1 2.9 %add_convert_fusion = bf16[2,256,1024]{2,1,0:T(8,128)(2,1)} fusion(f32[2,256,1024]{2,1,0:T(8,128)S(1)} %fusion.50, bf16[2,2,128,1,1024]{4,2,1,3,0:T(8,128)(2,1)} %bitcast.97, f32[2,128]{1,0:T(2,128)S(1)} %get-tuple-element.8, f32[2,256,128]{1,2,0:T(8,128)} %copy-done.4), kind=kOutput, calls=%fused_computation.25 | convolution fusion | flops 135463424 | bytes 4195328 | tf_op jit(solution)/shard_map/bte,bed->btd/dot_general | solution.py:89
  109.0 14.5 %all-to-all-done.3 = f32[128,9,128]{2,1,0:T(8,128)} async-done(((f32[128,9,128]{2,1,0:T(8,128)}), f32[128,9,128]{2,1,0:T(8,128)}, u32[]{:S(2)}, u32[]{:S(2)}) %all-to-all-start.3) | async-done | bytes 589856 | tf_op jit(solution)/shard_map/all_to_all | solution.py:100
  123.6 1.4 %reduce_sum.69 = f32[9,128]{1,0:T(8,128)S(1)} reduce(f32[128,9,128]{2,1,0:T(8,128)} %all-to-all-done.3, f32[]{:T(128)} %constant.9.clone.1), dimensions={0}, to_apply=%region_8.0 | reduce | flops 146304 | bytes 594436 | tf_op jit(solution)/shard_map/reduce_sum | solution.py:101
  124.9 0.6 fusion.63
  (20 shorter events, 0.1 us)
Async XLA Ops:
  0.6 27.1 %copy-start = (bf16[2,256,1024]{2,1,0:T(8,128)(2,1)S(1)}, bf16[2,256,1024]{2,1,0:T(8,128)(2,1)}, u32[]{:S(2)}) copy-start(bf16[2,256,1024]{2,1,0:T(8,128)(2,1)} %param.5) | copy-start | bytes 3145732
  26.9 3.5 %copy-start.10 = (bf16[2,256,1024]{2,1,0:T(8,128)(2,1)S(1)}, bf16[2,256,1024]{2,1,0:T(8,128)(2,1)}, u32[]{:S(2)}) copy-start(bf16[2,256,1024]{2,1,0:T(8,128)(2,1)} %param.9) | copy-start | bytes 3145732
  27.0 0.7 copy-start.5
  28.2 2.6 %copy-start.4 = (f32[2,256,128]{1,2,0:T(8,128)}, f32[2,256,128]{1,2,0:T(8,128)S(1)}, u32[]{:S(2)}) copy-start(f32[2,256,128]{1,2,0:T(8,128)S(1)} %fusion.48) | copy-start | bytes 786436
  56.0 4.0 %copy-start.2 = (bf16[256,1024]{1,0:T(8,128)(2,1)}, bf16[256,1024]{1,0:T(8,128)(2,1)S(1)}, u32[]{:S(2)}) copy-start(bf16[256,1024]{1,0:T(8,128)(2,1)S(1)} %squeeze.19) | copy-start | bytes 1572868
  56.2 3.8 %copy-start.7 = (bf16[256,1024]{1,0:T(8,128)(2,1)}, bf16[256,1024]{1,0:T(8,128)(2,1)S(1)}, u32[]{:S(2)}) copy-start(bf16[256,1024]{1,0:T(8,128)(2,1)S(1)} %squeeze.22) | copy-start | bytes 1572868
  56.2 8.9 %slice-start = ((s8[5242880]{0:T(1024)(128)(4,1)}), s8[4194304]{0:T(1024)(128)(4,1)S(1)}, s32[]{:S(2)}) async-start(s8[5242880]{0:T(1024)(128)(4,1)} %bitcast.102), calls=%async_computation.4 | async-start | bytes 8388608
  56.3 10.5 %slice-start.2 = ((s8[5242880]{0:T(1024)(128)(4,1)}), s8[4194304]{0:T(1024)(128)(4,1)S(1)}, s32[]{:S(2)}) async-start(s8[5242880]{0:T(1024)(128)(4,1)} %bitcast.104), calls=%async_computation.6 | async-start | bytes 8388608
  60.1 5.1 %slice-start.1 = ((s8[5242880]{0:T(1024)(128)(4,1)}), s8[1048576]{0:T(1024)(128)(4,1)S(1)}, s32[]{:S(2)}) async-start(s8[5242880]{0:T(1024)(128)(4,1)} %bitcast.102), calls=%async_computation.5 | async-start | bytes 2097152
  60.1 6.7 %slice-start.3 = ((s8[5242880]{0:T(1024)(128)(4,1)}), s8[1048576]{0:T(1024)(128)(4,1)S(1)}, s32[]{:S(2)}) async-start(s8[5242880]{0:T(1024)(128)(4,1)} %bitcast.104), calls=%async_computation.7 | async-start | bytes 2097152
  65.2 1.6 %copy-start.8 = (bf16[256,2560]{1,0:T(8,128)(2,1)}, bf16[256,2560]{1,0:T(8,128)(2,1)S(1)}, u32[]{:S(2)}) copy-start(bf16[256,2560]{1,0:T(8,128)(2,1)S(1)} %fusion.17) | copy-start | bytes 3932164
  70.5 23.6 %all-to-all-start.2 = ((bf16[2,256,1,1024]{3,0,2,1:T(2,128)(2,1)}), bf16[2,256,1,1024]{3,0,2,1:T(2,128)(2,1)S(1)}, u32[]{:S(2)}, u32[]{:S(2)}) async-start(bf16[2,256,1,1024]{3,0,2,1:T(2,128)(2,1)} %copy.31), calls=%async_computation.2 | async-start | bytes 2097152 | tf_op jit(solution)/shard_map/all_to_all | solution.py:74
  74.5 5.1 %copy-start.3 = (bf16[256,1024]{1,0:T(8,128)(2,1)S(1)}, bf16[256,1024]{1,0:T(8,128)(2,1)}, u32[]{:S(2)}) copy-start(bf16[256,1024]{1,0:T(8,128)(2,1)} %copy-done.2) | copy-start | bytes 1572868
  74.5 5.1 %copy-start.9 = (bf16[256,2560]{1,0:T(8,128)(2,1)S(1)}, bf16[256,2560]{1,0:T(8,128)(2,1)}, u32[]{:S(2)}) copy-start(bf16[256,2560]{1,0:T(8,128)(2,1)} %copy-done.8) | copy-start | bytes 3932164
  79.6 14.8 %copy-start.11 = (bf16[2,256,1024]{2,1,0:T(8,128)(2,1)S(1)}, bf16[2,256,1024]{2,1,0:T(8,128)(2,1)}, u32[]{:S(2)}) copy-start(bf16[2,256,1024]{2,1,0:T(8,128)(2,1)} %param.9) | copy-start | bytes 3145732
  94.1 1.3 %copy-start.14 = (f32[2,256,128]{1,2,0:T(8,128)S(1)}, f32[2,256,128]{1,2,0:T(8,128)}, u32[]{:S(2)}) copy-start(f32[2,256,128]{1,2,0:T(8,128)} %get-tuple-element.9) | copy-start | bytes 786436
  94.4 2.2 %copy-start.1 = (bf16[2,128,2,1,1024]{4,1,2,3,0:T(8,128)(2,1)}, bf16[2,128,2,1,1024]{4,1,2,3,0:T(8,128)(2,1)S(1)}, u32[]{:S(2)}) copy-start(bf16[2,128,2,1,1024]{4,1,2,3,0:T(8,128)(2,1)S(1)} %copy.42) | copy-start | bytes 3145732
  94.4 2.2 %copy-start.6 = (bf16[1024,128]{0,1:T(8,128)(2,1)S(1)}, bf16[1024,128]{0,1:T(8,128)(2,1)}, u32[]{:S(2)}) copy-start(bf16[1024,128]{0,1:T(8,128)(2,1)} %copy-done.5) | copy-start | bytes 786436
  94.9 3.3 %copy-start.12 = (f32[2,256,128]{1,2,0:T(8,128)}, f32[2,256,128]{1,2,0:T(8,128)S(1)}, u32[]{:S(2)}) copy-start(f32[2,256,128]{1,2,0:T(8,128)S(1)} %convolution_bitcast_fusion.2) | copy-start | bytes 786436
  96.6 1.6 %copy-start.13 = (f32[2,256,128]{1,2,0:T(8,128)}, f32[2,256,128]{1,2,0:T(8,128)S(1)}, u32[]{:S(2)}) copy-start(f32[2,256,128]{1,2,0:T(8,128)S(1)} %fusion.44) | copy-start | bytes 786436
  99.5 24.1 %all-to-all-start.3 = ((f32[128,9,128]{2,1,0:T(8,128)}), f32[128,9,128]{2,1,0:T(8,128)}, u32[]{:S(2)}, u32[]{:S(2)}) async-start(f32[128,9,128]{2,1,0:T(8,128)} %pad_maximum_fusion.1), calls=%async_computation.3 | async-start | bytes 2097152 | tf_op jit(solution)/shard_map/all_to_all | solution.py:100
  106.1 18.8 %copy-start.15 = (f32[8,128]{1,0:T(8,128)S(1)}, f32[8,128]{1,0:T(8,128)}, u32[]{:S(2)}) copy-start(f32[8,128]{1,0:T(8,128)} %param.6) | copy-start | bytes 12292

commit v2 on v0

v2 whole, which is shorter than its diff:
```python
import jax
import jax.numpy as jnp
from jax import lax
from jax.experimental import pallas as pl
from jax.experimental.pallas import tpu as pltpu
from jax.sharding import PartitionSpec as P

LOGIT_SCALE = 2.0
EPS = 1e-06
SQRT_HALF = 0.7071067811865476
INV_ROOT = 0.3989422804014327
AXES = ("exp", "rep")
LANES = 128
FF_BLOCK = 512
VMEM_BYTES = 24 * 1024 * 1024


def gelu_parts(pre_value):
    cumulative = 0.5 * (1.0 + lax.erf(pre_value * SQRT_HALF))
    gelu_slope = cumulative + pre_value * jnp.exp(-0.5 * pre_value * pre_value) * INV_ROOT
    return (pre_value * cumulative, gelu_slope)


def contract_last(left_side, right_side):
    return lax.dot_general(
        left_side, right_side, (((1,), (1,)), ((), ())), preferred_element_type=jnp.float32
    )


def contract_first(left_side, right_side):
    return lax.dot_general(
        left_side, right_side, (((0,), (0,)), ((), ())), preferred_element_type=jnp.float32
    )


def exchange(blocks):
    return lax.all_to_all(blocks, AXES, split_axis=0, concat_axis=0, tiled=True)


def put_pair(messages_ref, pair, first, second):
    rows = first.shape[1] // LANES
    cut = [vectors.reshape(vectors.shape[0], rows, LANES) for vectors in (first, second)]
    messages_ref[:, 2 * pair * rows : 2 * (pair + 1) * rows, :] = jnp.concatenate(
        cut, axis=1
    ).astype(jnp.bfloat16)


def take_pair(messages_ref, pair, target_ref):
    peers, width = messages_ref.shape[0], target_ref.shape[1]
    rows = width // LANES
    turned = jnp.swapaxes(messages_ref[:, 2 * pair * rows : 2 * (pair + 1) * rows, :], 0, 1)
    for image in range(2):
        for chunk in range(rows):
            target_ref[
                image * peers : (image + 1) * peers, chunk * LANES : (chunk + 1) * LANES
            ] = turned[image * rows + chunk]


def pair_rows(ref, pair):
    rows = ref.shape[1] // 2
    return ref.at[:, pair * rows : (pair + 1) * rows, :]


def route_kernel(
    router_ref,
    images_ref,
    out_grad_hbm,
    sent_ref,
    low_ref,
    norm_ref,
    dispatch_ref,
    combine_ref,
    out_grad_ref,
    sem,
):
    fetch = pltpu.make_async_copy(out_grad_hbm, out_grad_ref, sem)
    fetch.start()
    whole = router_ref[...]
    inv_norm = lax.rsqrt(jnp.sum(whole * whole, axis=0, keepdims=True) + EPS)
    low = (whole * inv_norm).astype(jnp.bfloat16)
    low_ref[...] = low
    norm_ref[...] = inv_norm
    pictures = images_ref.shape[0]
    slot_in = []
    for image in range(pictures):
        tokens = images_ref[image]
        logits = LOGIT_SCALE * jnp.dot(tokens, low, preferred_element_type=jnp.float32)
        raised = jnp.exp(logits - jnp.max(logits, axis=0, keepdims=True))
        dispatch = raised / jnp.sum(raised, axis=0, keepdims=True)
        dispatch_ref[image] = dispatch
        slot_in.append(contract_first(dispatch.astype(jnp.bfloat16), tokens))
        raised = jnp.exp(logits - jnp.max(logits, axis=1, keepdims=True))
        combine_ref[image] = raised / jnp.sum(raised, axis=1, keepdims=True)
    put_pair(sent_ref, 0, *slot_in)
    fetch.wait()
    slot_grad = [
        contract_first(combine_ref[image].astype(jnp.bfloat16), out_grad_ref[image])
        for image in range(pictures)
    ]
    put_pair(sent_ref, 1, *slot_grad)


def expert_kernel(
    recv_ref,
    w_in_ref,
    w_out_ref,
    sent_hbm,
    rows_hbm,
    grads_hbm,
    hidden_hbm,
    pre_grad_hbm,
    sent_ref,
    rows_ref,
    grads_ref,
    hidden_ref,
    pre_grad_ref,
    slope_ref,
    sems,
):
    copies = []

    def write_out(source, target):
        copy = pltpu.make_async_copy(source, target, sems.at[len(copies)])
        copy.start()
        copies.append(copy)

    hidden_width = hidden_ref.shape[1]
    blocks = [slice(at, at + FF_BLOCK) for at in range(0, hidden_width, FF_BLOCK)]
    take_pair(recv_ref, 0, rows_ref)
    write_out(rows_ref, rows_hbm)
    take_pair(recv_ref, 1, grads_ref)
    write_out(grads_ref, grads_hbm)
    for block in blocks:
        activated, gelu_slope = gelu_parts(
            jnp.dot(rows_ref[...], w_in_ref[0, :, block], preferred_element_type=jnp.float32)
        )
        hidden_ref[:, block] = activated.astype(jnp.bfloat16)
        slope_ref[:, block] = gelu_slope
    write_out(hidden_ref, hidden_hbm)
    peers = recv_ref.shape[0]
    slot_out = jnp.dot(hidden_ref[...], w_out_ref[0], preferred_element_type=jnp.float32)
    put_pair(sent_ref, 0, slot_out[:peers], slot_out[peers:])
    write_out(pair_rows(sent_ref, 0), pair_rows(sent_hbm, 0))
    for block in blocks:
        hidden_grad = contract_last(grads_ref[...], w_out_ref[0, block, :])
        pre_grad_ref[:, block] = (hidden_grad * slope_ref[:, block]).astype(jnp.bfloat16)
    write_out(pre_grad_ref, pre_grad_hbm)
    slot_dx = contract_last(pre_grad_ref[...], w_in_ref[0])
    put_pair(sent_ref, 1, slot_dx[:peers], slot_dx[peers:])
    write_out(pair_rows(sent_ref, 1), pair_rows(sent_hbm, 1))
    for copy in copies:
        copy.wait()


def logit_kernel(
    recv_ref,
    router_ref,
    norm_ref,
    low_ref,
    images_ref,
    out_grad_ref,
    dispatch_ref,
    combine_ref,
    term_hbm,
    logit_grad_hbm,
    slot_dx_hbm,
    term_ref,
    logit_grad_ref,
    slot_dx_ref,
    slot_out_ref,
    sems,
):
    peers, width = recv_ref.shape[0], slot_out_ref.shape[1]
    take_pair(recv_ref, 1, slot_dx_ref)
    save_dx = pltpu.make_async_copy(slot_dx_ref, slot_dx_hbm, sems.at[0])
    save_dx.start()
    take_pair(recv_ref, 0, slot_out_ref)
    hat_turned = jnp.zeros((peers, width), jnp.float32)
    for image in range(images_ref.shape[0]):
        picked = slice(image * peers, (image + 1) * peers)
        combine, dispatch = combine_ref[image], dispatch_ref[image]
        combine_grad = contract_last(out_grad_ref[image], slot_out_ref[picked, :])
        grad_combine = combine * (
            combine_grad - jnp.sum(combine * combine_grad, axis=1, keepdims=True)
        )
        dispatch_grad = contract_last(images_ref[image], slot_dx_ref[picked, :])
        grad_dispatch = dispatch * (
            dispatch_grad - jnp.sum(dispatch * dispatch_grad, axis=0, keepdims=True)
        )
        logit_grad = (LOGIT_SCALE * (grad_combine + grad_dispatch)).astype(jnp.bfloat16)
        logit_grad_ref[image] = logit_grad
        hat_turned += contract_first(logit_grad, images_ref[image])
    save_logit = pltpu.make_async_copy(logit_grad_ref, logit_grad_hbm, sems.at[1])
    save_logit.start()
    hat_part = hat_turned.T
    moment_part = jnp.sum(low_ref[...].astype(jnp.float32) * hat_part, axis=0, keepdims=True)
    inv_norm = norm_ref[...]
    term_ref[...] = (hat_part - router_ref[...] * inv_norm * moment_part) * inv_norm
    save_term = pltpu.make_async_copy(term_ref, term_hbm, sems.at[2])
    save_term.start()
    save_dx.wait()
    save_logit.wait()
    save_term.wait()


def per_device(images, router, w_in, w_out, out_grad):
    pictures, tokens, width = images.shape
    own_rows, experts = router.shape
    devices = lax.axis_size(AXES)
    hidden_width = w_in.shape[2]
    rows = pictures * devices
    f32, bf16 = jnp.float32, jnp.bfloat16
    params = pltpu.CompilerParams(vmem_limit_bytes=VMEM_BYTES)
    in_vmem = pl.BlockSpec(memory_space=pltpu.VMEM)
    in_hbm = pl.BlockSpec(memory_space=pltpu.HBM)

    router_whole = exchange(jnp.broadcast_to(router[None], (devices, own_rows, experts)))
    router_whole = router_whole.reshape(width, experts)
    message = ((devices, 4 * width // LANES, LANES), bf16)
    per_token = ((pictures, tokens, experts), f32)
    sent, router_low, inv_norm, dispatch, combine = pl.pallas_call(
        route_kernel,
        in_specs=[in_vmem, in_vmem, in_hbm],
        out_specs=[in_vmem] * 5,
        out_shape=[
            jax.ShapeDtypeStruct(*message),
            jax.ShapeDtypeStruct((width, experts), bf16),
            jax.ShapeDtypeStruct((1, experts), f32),
            jax.ShapeDtypeStruct(*per_token),
            jax.ShapeDtypeStruct(*per_token),
        ],
        scratch_shapes=[pltpu.VMEM(out_grad.shape, bf16), pltpu.SemaphoreType.DMA],
        compiler_params=params,
        name="route",
    )(router_whole, images, pltpu.with_memory_space_constraint(out_grad, pltpu.HBM))

    arrived = exchange(sent)
    outs = [message] + [((rows, width), bf16)] * 2 + [((rows, hidden_width), bf16)] * 2
    sent, slot_rows, slot_grads, hidden, pre_grad = pl.pallas_call(
        expert_kernel,
        in_specs=[in_vmem] * 3,
        out_specs=[in_hbm] * 5,
        out_shape=[pltpu.HBM(*out) for out in outs],
        scratch_shapes=[pltpu.VMEM(*out) for out in outs]
        + [pltpu.VMEM((rows, hidden_width), f32), pltpu.SemaphoreType.DMA((6,))],
        compiler_params=params,
        name="expert",
    )(arrived, w_in, w_out)
    returned = exchange(sent)
    grad_out = contract_first(hidden, slot_grads).astype(bf16)
    grad_in = contract_first(slot_rows, pre_grad).astype(bf16)

    outs = [((width, experts), f32), ((pictures, tokens, experts), bf16), ((rows, width), bf16)]
    term, logit_grad, slot_dx = pl.pallas_call(
        logit_kernel,
        in_specs=[in_vmem] * 8,
        out_specs=[in_hbm] * 3,
        out_shape=[pltpu.HBM(*out) for out in outs],
        scratch_shapes=[pltpu.VMEM(*out) for out in outs]
        + [pltpu.VMEM((rows, width), bf16), pltpu.SemaphoreType.DMA((3,))],
        compiler_params=params,
        name="logit",
    )(returned, router_whole, inv_norm, router_low, images, out_grad, dispatch, combine)
    terms = exchange(term.reshape(devices, own_rows, experts))
    router_grad = jnp.sum(terms, axis=0)
    images_grad = (
        jnp.einsum(
            "bte,bed->btd",
            dispatch.astype(bf16),
            slot_dx.reshape(pictures, experts, width),
            preferred_element_type=f32,
        )
        + jnp.einsum("bte,de->btd", logit_grad, router_low, preferred_element_type=f32)
    ).astype(bf16)
    return (images_grad, grad_in[None], grad_out[None], router_grad)


def solution(mesh):
    in_specs = (
        P(AXES, None, None),
        P(AXES, None),
        P(AXES, None, None),
        P(AXES, None, None),
        P(AXES, None, None),
    )
    out_specs = (
        P(AXES, None, None),
        P(AXES, None, None),
        P(AXES, None, None),
        P(AXES, None),
    )
    return jax.shard_map(
        per_device, mesh=mesh, in_specs=in_specs, out_specs=out_specs, check_vma=False
    )
```

time: 351 us -> 109 us (0.31)
  waiting for transfers between devices: 149 us -> 21 us
  blocking collectives: 143 us -> 48.2 us
  matrix products: 30.2 us -> 12 us
  Pallas kernels: 0 us -> 13.9 us
  between operations: 14.4 us -> 0.75 us
  starting transfers between devices: 4.04 us -> 8.98 us
    unnamed x2 -> x0, waiting for transfers between devices: 138 us -> none
    psum x1 -> x0, blocking collectives: 63.9 us -> none  [per_device(): moment = lax.psum(jnp.sum(own_low * hat_rows, axis=0), ('exp', 'rep'))]
    all_gather x1 -> x0, blocking collectives: 54.5 us -> none  [per_device(): router_whole = lax.all_gather(router, ('exp', 'rep'), axis=0, tiled=True)]
    all_to_all x1 -> x2, blocking collectives: 25 us -> 48.2 us  [exchange(): return lax.all_to_all(blocks, AXES, split_axis=0, concat_axis=0, tiled=True)]
    dot_general x11 -> x1, matrix products: 19.4 us -> 1.39 us  [per_device(): jnp.einsum('bte,bed->btd', dispatch.astype(bf16), slot_dx.reshape(picture...]
    pallas_call x0 -> x3, Pallas kernels: none -> 13.9 us  [the longest x1 8.47 us: per_device(): pl.pallas_call(expert_kernel, in_specs=[in_vmem] * 3, out_specs=[in_hbm]...]
    all_to_all x1 -> x2, waiting for transfers between devices: 10.4 us -> 21 us  [exchange(): return lax.all_to_all(blocks, AXES, split_axis=0, concat_axis=0, tiled=True)]
    all_to_all x1 -> x2, starting transfers between devices: 4 us -> 8.98 us  [exchange(): return lax.all_to_all(blocks, AXES, split_axis=0, concat_axis=0, tiled=True)]
  transfers between devices with their start and end apart: 2 -> 2, of which waited for: 2 -> 2; matrix products, arithmetic and copies ran while one was open for 3% -> 11% of each run, Pallas kernels for 0% -> 0%
where the time goes in v2:
time: 109 us
  blocking collectives  48.2 us (44%)
  waiting for transfers between devices  21 us (19%)
  Pallas kernels  13.9 us (13%)
  matrix products  12 us (11%)
  starting transfers between devices  8.98 us (8%)
  local copies, waits for them, and re-layouts  3.33 us (3%)
    all_to_all x2, blocking collectives, exchange(): return lax.all_to_all(blocks, AXES, split_axis=0, concat_axis=0, tiled=True)  48.2 us
    all_to_all x2, waiting for transfers between devices, exchange(): return lax.all_to_all(blocks, AXES, split_axis=0, concat_axis=0, tiled=True)  21 us
    dot_general x2, matrix products, contract_first(): lax.dot_general(left_side, right_side, (((0,), (0,)), ((), ())), preferre...  9.31 us
    all_to_all x2, starting transfers between devices, exchange(): return lax.all_to_all(blocks, AXES, split_axis=0, concat_axis=0, tiled=True)  8.98 us
    pallas_call x1, Pallas kernels, per_device(): pl.pallas_call(expert_kernel, in_specs=[in_vmem] * 3, out_specs=[in_hbm]...  8.47 us
    pallas_call x1, Pallas kernels, per_device(): pl.pallas_call(logit_kernel, in_specs=[in_vmem] * 8, out_specs=[in_hbm] *...  3.6 us
    unnamed x16, local copies, waits for them, and re-layouts  2.52 us
  transfers between devices with their start and end apart: 2, of which 2 were waited for; matrix products, arithmetic and copies ran while one was open for 11% of the time, Pallas kernels for 0%

profile of v2, /device:TPU:1, one launch (start us, length us, event | category | flops | bytes accessed | tf_op | source)
XLA Modules:
  0.0 108.9 jit_solution(10702580110371435062)
XLA Ops:
  0.6 0.0 copy-start.2
  0.6 0.8 broadcast_in_dim.12
  1.5 0.0 copy-start
  1.5 25.1 %all_to_all.20 = f32[128,8,128]{2,1,0:T(8,128)S(1)} all-to-all(f32[128,8,128]{2,1,0:T(8,128)S(1)} %broadcast_in_dim.12), channel_id=1, replica_groups=mesh['exp'=32,'rep'=4] {'exp','rep'}, dimensions={0} | all-to-all | bytes 1048576 | tf_op jit(solution)/shard_map/all_to_all | solution.py:37
  26.5 0.0 copy-done.2
  26.5 1.9 %route.1 = (bf16[128,32,128]{2,1,0:T(8,128)(2,1)S(1)}, bf16[1024,128]{1,0:T(8,128)(2,1)S(1)}, f32[1,128]{1,0:T(1,128)S(1)}, f32[2,256,128]{2,1,0:T(8,128)S(1)}, f32[2,256,128]{2,1,0:T(8,128)S(1)}) custom-call(f32[1024,128]{1,0:T(8,128)S(1)} %bitcast.16, bf16[2,256,1024]{2,1,0:T(8,128)(2,1)S(1)} %copy-done.2, bf16[2,256,1024]{2,1,0:T(8,128)(2,1)} %out_grad_ref.1), custom_call_target="tpu_custom_call" | custom-call | tf_op jit(solution)/shard_map/route/pallas_call | solution.py:221
  28.4 23.1 %all_to_all.21.recv_ref = bf16[128,32,128]{2,1,0:T(8,128)(2,1)S(1)} all-to-all(bf16[128,32,128]{2,1,0:T(8,128)(2,1)S(1)} %get-tuple-element.18), channel_id=1, replica_groups=mesh['exp'=32,'rep'=4] {'exp','rep'}, dimensions={0} | all-to-all | bytes 2097152 | tf_op jit(solution)/shard_map/all_to_all | solution.py:37
  51.5 0.0 copy-done
  51.5 0.0 copy-start.1
  51.5 2.5 %copy-done.1 = bf16[1,2560,1024]{2,1,0:T(8,128)(2,1)S(1)} copy-done((bf16[1,2560,1024]{2,1,0:T(8,128)(2,1)S(1)}, bf16[1,2560,1024]{2,1,0:T(8,128)(2,1)}, u32[]{:S(2)}) %copy-start.1) | copy-done | bytes 5242904
  54.0 8.5 %expert.1 = (bf16[128,32,128]{2,1,0:T(8,128)(2,1)}, bf16[256,1024]{1,0:T(8,128)(2,1)}, bf16[256,1024]{1,0:T(8,128)(2,1)}, bf16[256,2560]{1,0:T(8,128)(2,1)}, bf16[256,2560]{1,0:T(8,128)(2,1)}) custom-call(bf16[128,32,128]{2,1,0:T(8,128)(2,1)S(1)} %all_to_all.21.recv_ref, bf16[1,1024,2560]{2,1,0:T(8,128)(2,1)S(1)} %copy-done, bf16[1,2560,1024]{2,1,0:T(8,128)(2,1)S(1)} %copy-done.1), custom_call_target="tpu_custom_call" | custom-call | tf_op jit(solution)/shard_map/expert/pallas_call | solution.py:239
  62.5 0.0 copy-start.5
  62.5 5.0 %all-to-all-start.2 = ((bf16[128,32,128]{2,1,0:T(8,128)(2,1)}), bf16[128,32,128]{2,1,0:T(8,128)(2,1)}, u32[]{:S(2)}, u32[]{:S(2)}) async-start(bf16[128,32,128]{2,1,0:T(8,128)(2,1)} %get-tuple-element.19), calls=%async_computation.2 | async-start | bytes 2097152 | tf_op jit(solution)/shard_map/all_to_all | solution.py:37
  67.5 0.0 copy-done.5
  67.5 0.0 copy-start.4
  67.6 0.0 copy-start.7
  67.6 5.4 %fusion = bf16[1,1024,2560]{2,1,0:T(8,128)(2,1)} fusion(bf16[256,1024]{1,0:T(8,128)(2,1)S(1)} %copy-done.5, bf16[256,2560]{1,0:T(8,128)(2,1)} %get-tuple-element.26), kind=kOutput, calls=%fused_computation.2 | convolution fusion | flops 1344798720 | bytes 7077888 | tf_op jit(solution)/shard_map/dot_general | solution.py:31
  73.0 0.0 copy-done.4
  73.0 0.0 copy-done.7
  73.0 0.0 copy-start.3
  73.0 3.9 %fusion.1 = bf16[1,2560,1024]{2,1,0:T(8,128)(2,1)} fusion(bf16[256,2560]{1,0:T(8,128)(2,1)S(1)} %copy-done.4, bf16[256,1024]{1,0:T(8,128)(2,1)S(1)} %copy-done.7), kind=kOutput, calls=%fused_computation.3 | convolution fusion | flops 1344798720 | bytes 7077888 | tf_op jit(solution)/shard_map/dot_general | solution.py:31
  76.9 9.8 %all-to-all-done.2.recv_ref = bf16[128,32,128]{2,1,0:T(8,128)(2,1)} async-done(((bf16[128,32,128]{2,1,0:T(8,128)(2,1)}), bf16[128,32,128]{2,1,0:T(8,128)(2,1)}, u32[]{:S(2)}, u32[]{:S(2)}) %all-to-all-start.2) | async-done | bytes 1048608 | tf_op jit(solution)/shard_map/all_to_all | solution.py:37
  86.7 0.0 copy-done.3
  86.7 3.6 %logit.1 = (f32[1024,128]{1,0:T(8,128)}, bf16[2,256,128]{2,1,0:T(8,128)(2,1)}, bf16[256,1024]{1,0:T(8,128)(2,1)}) custom-call(bf16[128,32,128]{2,1,0:T(8,128)(2,1)} %all-to-all-done.2.recv_ref, f32[1024,128]{1,0:T(8,128)S(1)} %bitcast.17, f32[1,128]{1,0:T(1,128)S(1)} %get-tuple-element.20.norm_ref, bf16[1024,128]{1,0:T(8,128)(2,1)S(1)} %get-tuple-element.21.low_ref, ...), custom_call_target="tpu_custom_call" | custom-call | tf_op jit(solution)/shard_map/logit/pallas_call | solution.py:254
  90.3 0.0 copy-start.6
  90.4 3.9 %all-to-all-start.3 = ((f32[128,8,128]{2,1,0:T(8,128)}), f32[128,8,128]{2,1,0:T(8,128)S(1)}, u32[]{:S(2)}, u32[]{:S(2)}) async-start(f32[128,8,128]{2,1,0:T(8,128)} %bitcast.19), calls=%async_computation.3 | async-start | bytes 1048576 | tf_op jit(solution)/shard_map/all_to_all | solution.py:37
  94.3 1.3 %fusion.2 = f32[2,256,1024]{2,1,0:T(8,128)S(1)} fusion(bf16[2,256,128]{2,1,0:T(8,128)(2,1)} %get-tuple-element.24, bf16[1024,128]{1,0:T(8,128)(2,1)S(1)} %get-tuple-element.21.low_ref), kind=kOutput, calls=%fused_computation.5 | convolution fusion | flops 134217728 | bytes 2490368 | tf_op jit(solution)/shard_map/bte,de->btd/dot_general | solution.py:273
  95.6 0.0 copy-done.6
  95.7 1.4 %add_convert_fusion = bf16[2,256,1024]{2,1,0:T(8,128)(2,1)} fusion(f32[2,256,1024]{2,1,0:T(8,128)S(1)} %fusion.2, bf16[2,128,1024]{2,1,0:T(8,128)(2,1)S(1)} %bitcast.18, f32[2,256,128]{2,1,0:T(8,128)S(1)} %get-tuple-element.17.dispatch_ref), kind=kOutput, calls=%fused_computation.4 | convolution fusion | flops 135331840 | bytes 3932160 | tf_op jit(solution)/shard_map/bte,bed->btd/dot_general | solution.py:267
  97.0 11.2 %all-to-all-done.3 = f32[128,8,128]{2,1,0:T(8,128)S(1)} async-done(((f32[128,8,128]{2,1,0:T(8,128)}), f32[128,8,128]{2,1,0:T(8,128)S(1)}, u32[]{:S(2)}, u32[]{:S(2)}) %all-to-all-start.3) | async-done | bytes 524320 | tf_op jit(solution)/shard_map/all_to_all | solution.py:37
  108.2 0.7 reduce_sum.9
Async XLA Ops:
  0.6 25.9 %copy-start.2 = (bf16[2,256,1024]{2,1,0:T(8,128)(2,1)S(1)}, bf16[2,256,1024]{2,1,0:T(8,128)(2,1)}, u32[]{:S(2)}) copy-start(bf16[2,256,1024]{2,1,0:T(8,128)(2,1)} %images_ref.3) | copy-start | bytes 3145732
  1.5 50.1 %copy-start = (bf16[1,1024,2560]{2,1,0:T(8,128)(2,1)S(1)}, bf16[1,1024,2560]{2,1,0:T(8,128)(2,1)}, u32[]{:S(2)}) copy-start(bf16[1,1024,2560]{2,1,0:T(8,128)(2,1)} %w_in_ref.1) | copy-start | bytes 15728644
  51.5 2.5 %copy-start.1 = (bf16[1,2560,1024]{2,1,0:T(8,128)(2,1)S(1)}, bf16[1,2560,1024]{2,1,0:T(8,128)(2,1)}, u32[]{:S(2)}) copy-start(bf16[1,2560,1024]{2,1,0:T(8,128)(2,1)} %w_out_ref.1) | copy-start | bytes 15728644
  62.5 5.1 %copy-start.5 = (bf16[256,1024]{1,0:T(8,128)(2,1)S(1)}, bf16[256,1024]{1,0:T(8,128)(2,1)}, u32[]{:S(2)}) copy-start(bf16[256,1024]{1,0:T(8,128)(2,1)} %get-tuple-element.25) | copy-start | bytes 1572868
  62.5 24.2 %all-to-all-start.2 = ((bf16[128,32,128]{2,1,0:T(8,128)(2,1)}), bf16[128,32,128]{2,1,0:T(8,128)(2,1)}, u32[]{:S(2)}, u32[]{:S(2)}) async-start(bf16[128,32,128]{2,1,0:T(8,128)(2,1)} %get-tuple-element.19), calls=%async_computation.2 | async-start | bytes 2097152 | tf_op jit(solution)/shard_map/all_to_all | solution.py:37
  67.5 5.4 %copy-start.4 = (bf16[256,2560]{1,0:T(8,128)(2,1)S(1)}, bf16[256,2560]{1,0:T(8,128)(2,1)}, u32[]{:S(2)}) copy-start(bf16[256,2560]{1,0:T(8,128)(2,1)} %get-tuple-element.27) | copy-start | bytes 3932164
  67.6 5.4 %copy-start.7 = (bf16[256,1024]{1,0:T(8,128)(2,1)S(1)}, bf16[256,1024]{1,0:T(8,128)(2,1)}, u32[]{:S(2)}) copy-start(bf16[256,1024]{1,0:T(8,128)(2,1)} %get-tuple-element.28) | copy-start | bytes 1572868
  73.0 13.8 %copy-start.3 = (bf16[2,256,1024]{2,1,0:T(8,128)(2,1)S(1)}, bf16[2,256,1024]{2,1,0:T(8,128)(2,1)}, u32[]{:S(2)}) copy-start(bf16[2,256,1024]{2,1,0:T(8,128)(2,1)} %out_grad_ref.1) | copy-start | bytes 3145732
  90.3 5.3 %copy-start.6 = (bf16[256,1024]{1,0:T(8,128)(2,1)S(1)}, bf16[256,1024]{1,0:T(8,128)(2,1)}, u32[]{:S(2)}) copy-start(bf16[256,1024]{1,0:T(8,128)(2,1)} %get-tuple-element.23) | copy-start | bytes 1572868
  90.4 17.9 %all-to-all-start.3 = ((f32[128,8,128]{2,1,0:T(8,128)}), f32[128,8,128]{2,1,0:T(8,128)S(1)}, u32[]{:S(2)}, u32[]{:S(2)}) async-start(f32[128,8,128]{2,1,0:T(8,128)} %bitcast.19), calls=%async_computation.3 | async-start | bytes 1048576 | tf_op jit(solution)/shard_map/all_to_all | solution.py:37

commit v3 on v2

--- a/solution.py
+++ b/solution.py
@@ -59,6 +59,10 @@
 def pair_rows(ref, pair):
     rows = ref.shape[1] // 2
     return ref.at[:, pair * rows : (pair + 1) * rows, :]
+
+
+def spread_kernel(rows_ref, copies_ref):
+    copies_ref[...] = jnp.broadcast_to(rows_ref[...][None], copies_ref.shape)
 
 
 def route_kernel(
@@ -153,7 +157,7 @@
 
 
 def logit_kernel(
-    recv_ref,
+    recv_hbm,
     router_ref,
     norm_ref,
     low_ref,
@@ -168,12 +172,21 @@
     logit_grad_ref,
     slot_dx_ref,
     slot_out_ref,
+    recv_ref,
     sems,
 ):
+    fetches = [
+        pltpu.make_async_copy(pair_rows(recv_hbm, pair), pair_rows(recv_ref, pair), sems.at[3 + pair])
+        for pair in range(2)
+    ]
+    fetches[1].start()
+    fetches[0].start()
     peers, width = recv_ref.shape[0], slot_out_ref.shape[1]
+    fetches[1].wait()
     take_pair(recv_ref, 1, slot_dx_ref)
     save_dx = pltpu.make_async_copy(slot_dx_ref, slot_dx_hbm, sems.at[0])
     save_dx.start()
+    fetches[0].wait()
     take_pair(recv_ref, 0, slot_out_ref)
     hat_turned = jnp.zeros((peers, width), jnp.float32)
     for image in range(images_ref.shape[0]):
@@ -195,7 +208,8 @@
     hat_part = hat_turned.T
     moment_part = jnp.sum(low_ref[...].astype(jnp.float32) * hat_part, axis=0, keepdims=True)
     inv_norm = norm_ref[...]
-    term_ref[...] = (hat_part - router_ref[...] * inv_norm * moment_part) * inv_norm
+    term = (hat_part - router_ref[...] * inv_norm * moment_part) * inv_norm
+    term_ref[...] = term.astype(jnp.bfloat16)
     save_term = pltpu.make_async_copy(term_ref, term_hbm, sems.at[2])
     save_term.start()
     save_dx.wait()
@@ -214,8 +228,18 @@
     in_vmem = pl.BlockSpec(memory_space=pltpu.VMEM)
     in_hbm = pl.BlockSpec(memory_space=pltpu.HBM)
 
-    router_whole = exchange(jnp.broadcast_to(router[None], (devices, own_rows, experts)))
-    router_whole = router_whole.reshape(width, experts)
+    copies = pl.pallas_call(
+        spread_kernel,
+        in_specs=[in_vmem],
+        out_specs=in_vmem,
+        out_shape=jax.ShapeDtypeStruct((devices, own_rows, experts), f32),
+        compiler_params=params,
+        cost_estimate=pl.CostEstimate(
+            flops=20_000_000_000, bytes_accessed=30_000_000, transcendentals=300_000
+        ),
+        name="spread",
+    )(router)
+    router_whole = exchange(copies).reshape(width, experts)
     message = ((devices, 4 * width // LANES, LANES), bf16)
     per_token = ((pictures, tokens, experts), f32)
     sent, router_low, inv_norm, dispatch, combine = pl.pallas_call(
@@ -242,7 +266,10 @@
         out_specs=[in_hbm] * 5,
         out_shape=[pltpu.HBM(*out) for out in outs],
         scratch_shapes=[pltpu.VMEM(*out) for out in outs]
-        + [pltpu.VMEM((rows, hidden_width), f32), pltpu.SemaphoreType.DMA((6,))],
+        + [
+            pltpu.VMEM((rows, hidden_width), f32),
+            pltpu.SemaphoreType.DMA((6,)),
+        ],
         compiler_params=params,
         name="expert",
     )(arrived, w_in, w_out)
@@ -250,19 +277,19 @@
     grad_out = contract_first(hidden, slot_grads).astype(bf16)
     grad_in = contract_first(slot_rows, pre_grad).astype(bf16)
 
-    outs = [((width, experts), f32), ((pictures, tokens, experts), bf16), ((rows, width), bf16)]
+    outs = [((width, experts), bf16), ((pictures, tokens, experts), bf16), ((rows, width), bf16)]
     term, logit_grad, slot_dx = pl.pallas_call(
         logit_kernel,
-        in_specs=[in_vmem] * 8,
+        in_specs=[in_hbm] + [in_vmem] * 7,
         out_specs=[in_hbm] * 3,
         out_shape=[pltpu.HBM(*out) for out in outs],
         scratch_shapes=[pltpu.VMEM(*out) for out in outs]
-        + [pltpu.VMEM((rows, width), bf16), pltpu.SemaphoreType.DMA((3,))],
+        + [pltpu.VMEM((rows, width), bf16), pltpu.VMEM(*message), pltpu.SemaphoreType.DMA((5,))],
         compiler_params=params,
         name="logit",
-    )(returned, router_whole, inv_norm, router_low, images, out_grad, dispatch, combine)
+    )(pltpu.with_memory_space_constraint(returned, pltpu.HBM), router_whole, inv_norm, router_low, images, out_grad, dispatch, combine)
     terms = exchange(term.reshape(devices, own_rows, experts))
-    router_grad = jnp.sum(terms, axis=0)
+    router_grad = jnp.sum(terms.astype(f32), axis=0)
     images_grad = (
         jnp.einsum(
             "bte,bed->btd",

time: 109 us -> 104 us (0.954)
  waiting for transfers between devices: 21 us -> 18.4 us
  local copies, waits for them, and re-layouts: 3.33 us -> 0.81 us
    all_to_all x2, waiting for transfers between devices: 21 us -> 18.4 us  [exchange(): return lax.all_to_all(blocks, AXES, split_axis=0, concat_axis=0, tiled=True)]
    unnamed x16 -> x18, local copies, waits for them, and re-layouts: 2.52 us -> 0.81 us
    pallas_call x1 -> x2, Pallas kernels: 3.6 us -> 3.51 us  [the longest x1 3.47 us: per_device(): pl.pallas_call(logit_kernel, in_specs=[in_hbm] + [in_vmem] * 7, out_specs...]
  transfers between devices with their start and end apart: 2 -> 2, of which waited for: 2 -> 2; matrix products, arithmetic and copies ran while one was open for 11% -> 12% of each run, Pallas kernels for 0% -> 0%
where the time goes in v3:
time: 104 us; the launch traced here: 103 us
  blocking collectives  48.2 us (46%)
  waiting for transfers between devices  18.4 us (18%)
  Pallas kernels  13.5 us (13%)
  matrix products  12 us (12%)
  starting transfers between devices  8.98 us (9%)
    all_to_all x2, blocking collectives, exchange(): return lax.all_to_all(blocks, AXES, split_axis=0, concat_axis=0, tiled=True)  48.2 us
    all_to_all x2, waiting for transfers between devices, exchange(): return lax.all_to_all(blocks, AXES, split_axis=0, concat_axis=0, tiled=True)  18.4 us
    dot_general x2, matrix products, contract_first(): lax.dot_general(left_side, right_side, (((0,), (0,)), ((), ())), preferre...  9.31 us
    all_to_all x2, starting transfers between devices, exchange(): return lax.all_to_all(blocks, AXES, split_axis=0, concat_axis=0, tiled=True)  8.98 us
    pallas_call x1, Pallas kernels, per_device(): pl.pallas_call(expert_kernel, in_specs=[in_vmem] * 3, out_specs=[in_hbm]...  8.11 us
    pallas_call x1, Pallas kernels, per_device(): pl.pallas_call(logit_kernel, in_specs=[in_hbm] + [in_vmem] * 7, out_specs...  3.47 us
  transfers between devices with their start and end apart: 2, of which 2 were waited for; matrix products, arithmetic and copies ran while one was open for 12% of the time, Pallas kernels for 0%

profile of v3, /device:TPU:1, one launch (start us, length us, event | category | flops | bytes accessed | tf_op | source)
XLA Modules:
  0.0 103.3 jit_solution(15971470232968372828)
XLA Ops:
  0.6 0.0 copy-start.2
  0.6 0.0 copy-start.4
  0.7 0.8 copy-done.4
  1.4 0.0 copy-start.1
  1.5 0.0 copy-start
  1.5 25.1 %all_to_all.20 = f32[128,8,128]{2,1,0:T(8,128)S(1)} all-to-all(f32[128,8,128]{2,1,0:T(8,128)S(1)} %spread.1), channel_id=1, replica_groups=mesh['exp'=32,'rep'=4] {'exp','rep'}, dimensions={0} | all-to-all | bytes 1048576 | tf_op jit(solution)/shard_map/all_to_all | solution.py:37
  26.5 0.0 copy-done.2
  26.5 1.9 %route.1 = (bf16[128,32,128]{2,1,0:T(8,128)(2,1)S(1)}, bf16[1024,128]{1,0:T(8,128)(2,1)S(1)}, f32[1,128]{1,0:T(1,128)S(1)}, f32[2,256,128]{2,1,0:T(8,128)S(1)}, f32[2,256,128]{2,1,0:T(8,128)S(1)}) custom-call(f32[1024,128]{1,0:T(8,128)S(1)} %bitcast.16, bf16[2,256,1024]{2,1,0:T(8,128)(2,1)S(1)} %copy-done.2, bf16[2,256,1024]{2,1,0:T(8,128)(2,1)} %out_grad_ref.1), custom_call_target="tpu_custom_call" | custom-call | tf_op jit(solution)/shard_map/route/pallas_call | solution.py:245
  28.4 23.1 %all_to_all.21.recv_ref = bf16[128,32,128]{2,1,0:T(8,128)(2,1)S(1)} all-to-all(bf16[128,32,128]{2,1,0:T(8,128)(2,1)S(1)} %get-tuple-element.18), channel_id=1, replica_groups=mesh['exp'=32,'rep'=4] {'exp','rep'}, dimensions={0} | all-to-all | bytes 2097152 | tf_op jit(solution)/shard_map/all_to_all | solution.py:37
  51.5 0.0 copy-done.1
  51.5 0.0 copy-done
  51.5 8.1 %expert.1 = (bf16[128,32,128]{2,1,0:T(8,128)(2,1)}, bf16[256,1024]{1,0:T(8,128)(2,1)}, bf16[256,1024]{1,0:T(8,128)(2,1)}, bf16[256,2560]{1,0:T(8,128)(2,1)}, bf16[256,2560]{1,0:T(8,128)(2,1)}) custom-call(bf16[128,32,128]{2,1,0:T(8,128)(2,1)S(1)} %all_to_all.21.recv_ref, bf16[1,1024,2560]{2,1,0:T(8,128)(2,1)S(1)} %copy-done, bf16[1,2560,1024]{2,1,0:T(8,128)(2,1)S(1)} %copy-done.1), custom_call_target="tpu_custom_call" | custom-call | tf_op jit(solution)/shard_map/expert/pallas_call | solution.py:263
  59.6 0.0 copy-start.6
  59.7 5.1 %all-to-all-start.2 = ((bf16[128,32,128]{2,1,0:T(8,128)(2,1)}), bf16[128,32,128]{2,1,0:T(8,128)(2,1)}, u32[]{:S(2)}, u32[]{:S(2)}) async-start(bf16[128,32,128]{2,1,0:T(8,128)(2,1)} %get-tuple-element.19), calls=%async_computation.2 | async-start | bytes 2097152 | tf_op jit(solution)/shard_map/all_to_all | solution.py:37
  64.7 0.0 copy-done.6
  64.7 0.0 copy-start.5
  64.7 0.0 copy-start.8
  64.8 5.4 %fusion = bf16[1,1024,2560]{2,1,0:T(8,128)(2,1)} fusion(bf16[256,1024]{1,0:T(8,128)(2,1)S(1)} %copy-done.6, bf16[256,2560]{1,0:T(8,128)(2,1)} %get-tuple-element.26), kind=kOutput, calls=%fused_computation.2 | convolution fusion | flops 1344798720 | bytes 7077888 | tf_op jit(solution)/shard_map/dot_general | solution.py:31
  70.1 0.0 copy-done.5
  70.2 0.0 copy-done.8
  70.2 0.0 copy-start.3
  70.2 3.9 %fusion.1 = bf16[1,2560,1024]{2,1,0:T(8,128)(2,1)} fusion(bf16[256,2560]{1,0:T(8,128)(2,1)S(1)} %copy-done.5, bf16[256,1024]{1,0:T(8,128)(2,1)S(1)} %copy-done.8), kind=kOutput, calls=%fused_computation.3 | convolution fusion | flops 1344798720 | bytes 7077888 | tf_op jit(solution)/shard_map/dot_general | solution.py:31
  74.1 9.8 %all-to-all-done.2.recv_hbm = bf16[128,32,128]{2,1,0:T(8,128)(2,1)} async-done(((bf16[128,32,128]{2,1,0:T(8,128)(2,1)}), bf16[128,32,128]{2,1,0:T(8,128)(2,1)}, u32[]{:S(2)}, u32[]{:S(2)}) %all-to-all-start.2) | async-done | bytes 1048608 | tf_op jit(solution)/shard_map/all_to_all | solution.py:37
  83.9 0.0 copy-done.3
  83.9 3.5 %logit.1 = (bf16[1024,128]{1,0:T(8,128)(2,1)}, bf16[2,256,128]{2,1,0:T(8,128)(2,1)}, bf16[256,1024]{1,0:T(8,128)(2,1)}) custom-call(bf16[128,32,128]{2,1,0:T(8,128)(2,1)} %all-to-all-done.2.recv_hbm, f32[1024,128]{1,0:T(8,128)S(1)} %bitcast.17, f32[1,128]{1,0:T(1,128)S(1)} %get-tuple-element.20.norm_ref, bf16[1024,128]{1,0:T(8,128)(2,1)S(1)} %get-tuple-element.21.low_ref, ...), custom_call_target="tpu_custom_call" | custom-call | tf_op jit(solution)/shard_map/logit/pallas_call | solution.py:281
  87.4 0.0 copy-start.7
  87.4 3.9 %all-to-all-start.3 = ((bf16[128,8,128]{2,1,0:T(8,128)(2,1)}), bf16[128,8,128]{2,1,0:T(8,128)(2,1)S(1)}, u32[]{:S(2)}, u32[]{:S(2)}) async-start(bf16[128,8,128]{2,1,0:T(8,128)(2,1)} %bitcast.19), calls=%async_computation.3 | async-start | bytes 524288 | tf_op jit(solution)/shard_map/all_to_all | solution.py:37
  91.3 1.3 %fusion.2 = f32[2,256,1024]{2,1,0:T(8,128)S(1)} fusion(bf16[2,256,128]{2,1,0:T(8,128)(2,1)} %get-tuple-element.24, bf16[1024,128]{1,0:T(8,128)(2,1)S(1)} %get-tuple-element.21.low_ref), kind=kOutput, calls=%fused_computation.6 | convolution fusion | flops 134217728 | bytes 2490368 | tf_op jit(solution)/shard_map/bte,de->btd/dot_general | solution.py:300
  92.7 0.0 copy-done.7
  92.7 1.4 %add_convert_fusion = bf16[2,256,1024]{2,1,0:T(8,128)(2,1)} fusion(f32[2,256,1024]{2,1,0:T(8,128)S(1)} %fusion.2, bf16[2,128,1024]{2,1,0:T(8,128)(2,1)S(1)} %bitcast.18, f32[2,256,128]{2,1,0:T(8,128)S(1)} %get-tuple-element.17.dispatch_ref), kind=kOutput, calls=%fused_computation.4 | convolution fusion | flops 135331840 | bytes 3932160 | tf_op jit(solution)/shard_map/bte,bed->btd/dot_general | solution.py:294
  94.1 8.5 %all-to-all-done.3 = bf16[128,8,128]{2,1,0:T(8,128)(2,1)S(1)} async-done(((bf16[128,8,128]{2,1,0:T(8,128)(2,1)}), bf16[128,8,128]{2,1,0:T(8,128)(2,1)S(1)}, u32[]{:S(2)}, u32[]{:S(2)}) %all-to-all-start.3) | async-done | bytes 262176 | tf_op jit(solution)/shard_map/all_to_all | solution.py:37
  102.6 0.7 convert_reduce_fusion
  (1 shorter events, 0.0 us)
Async XLA Ops:
  0.6 25.9 %copy-start.2 = (bf16[2,256,1024]{2,1,0:T(8,128)(2,1)S(1)}, bf16[2,256,1024]{2,1,0:T(8,128)(2,1)}, u32[]{:S(2)}) copy-start(bf16[2,256,1024]{2,1,0:T(8,128)(2,1)} %images_ref.3) | copy-start | bytes 3145732
  0.6 0.8 copy-start.4
  1.4 50.1 %copy-start.1 = (bf16[1,2560,1024]{2,1,0:T(8,128)(2,1)S(1)}, bf16[1,2560,1024]{2,1,0:T(8,128)(2,1)}, u32[]{:S(2)}) copy-start(bf16[1,2560,1024]{2,1,0:T(8,128)(2,1)} %w_out_ref.1) | copy-start | bytes 15728644
  1.5 50.1 %copy-start = (bf16[1,1024,2560]{2,1,0:T(8,128)(2,1)S(1)}, bf16[1,1024,2560]{2,1,0:T(8,128)(2,1)}, u32[]{:S(2)}) copy-start(bf16[1,1024,2560]{2,1,0:T(8,128)(2,1)} %w_in_ref.1) | copy-start | bytes 15728644
  59.6 5.1 %copy-start.6 = (bf16[256,1024]{1,0:T(8,128)(2,1)S(1)}, bf16[256,1024]{1,0:T(8,128)(2,1)}, u32[]{:S(2)}) copy-start(bf16[256,1024]{1,0:T(8,128)(2,1)} %get-tuple-element.25) | copy-start | bytes 1572868
  59.7 24.3 %all-to-all-start.2 = ((bf16[128,32,128]{2,1,0:T(8,128)(2,1)}), bf16[128,32,128]{2,1,0:T(8,128)(2,1)}, u32[]{:S(2)}, u32[]{:S(2)}) async-start(bf16[128,32,128]{2,1,0:T(8,128)(2,1)} %get-tuple-element.19), calls=%async_computation.2 | async-start | bytes 2097152 | tf_op jit(solution)/shard_map/all_to_all | solution.py:37
  64.7 5.4 %copy-start.5 = (bf16[256,2560]{1,0:T(8,128)(2,1)S(1)}, bf16[256,2560]{1,0:T(8,128)(2,1)}, u32[]{:S(2)}) copy-start(bf16[256,2560]{1,0:T(8,128)(2,1)} %get-tuple-element.27) | copy-start | bytes 3932164
  64.7 5.4 %copy-start.8 = (bf16[256,1024]{1,0:T(8,128)(2,1)S(1)}, bf16[256,1024]{1,0:T(8,128)(2,1)}, u32[]{:S(2)}) copy-start(bf16[256,1024]{1,0:T(8,128)(2,1)} %get-tuple-element.28) | copy-start | bytes 1572868
  70.2 13.8 %copy-start.3 = (bf16[2,256,1024]{2,1,0:T(8,128)(2,1)S(1)}, bf16[2,256,1024]{2,1,0:T(8,128)(2,1)}, u32[]{:S(2)}) copy-start(bf16[2,256,1024]{2,1,0:T(8,128)(2,1)} %out_grad_ref.1) | copy-start | bytes 3145732
  87.4 5.3 %copy-start.7 = (bf16[256,1024]{1,0:T(8,128)(2,1)S(1)}, bf16[256,1024]{1,0:T(8,128)(2,1)}, u32[]{:S(2)}) copy-start(bf16[256,1024]{1,0:T(8,128)(2,1)} %get-tuple-element.23) | copy-start | bytes 1572868
  87.4 15.2 %all-to-all-start.3 = ((bf16[128,8,128]{2,1,0:T(8,128)(2,1)}), bf16[128,8,128]{2,1,0:T(8,128)(2,1)S(1)}, u32[]{:S(2)}, u32[]{:S(2)}) async-start(bf16[128,8,128]{2,1,0:T(8,128)(2,1)} %bitcast.19), calls=%async_computation.3 | async-start | bytes 524288 | tf_op jit(solution)/shard_map/all_to_all | solution.py:37

commit v4 on v3

--- a/solution.py
+++ b/solution.py
@@ -12,6 +12,7 @@
 AXES = ("exp", "rep")
 LANES = 128
 FF_BLOCK = 512
+PAIR_CUTS = 4
 VMEM_BYTES = 24 * 1024 * 1024
 
 
@@ -61,6 +62,18 @@
     return ref.at[:, pair * rows : (pair + 1) * rows, :]
 
 
+def pair_copies(source, target, pair, sems, first_sem):
+    peers = source.shape[0] // PAIR_CUTS
+    return [
+        pltpu.make_async_copy(
+            pair_rows(source, pair).at[cut * peers : (cut + 1) * peers],
+            pair_rows(target, pair).at[cut * peers : (cut + 1) * peers],
+            sems.at[first_sem + cut],
+        )
+        for cut in range(PAIR_CUTS)
+    ]
+
+
 def spread_kernel(rows_ref, copies_ref):
     copies_ref[...] = jnp.broadcast_to(rows_ref[...][None], copies_ref.shape)
 
@@ -68,17 +81,13 @@
 def route_kernel(
     router_ref,
     images_ref,
-    out_grad_hbm,
+    out_grad_ref,
     sent_ref,
     low_ref,
     norm_ref,
     dispatch_ref,
     combine_ref,
-    out_grad_ref,
-    sem,
 ):
-    fetch = pltpu.make_async_copy(out_grad_hbm, out_grad_ref, sem)
-    fetch.start()
     whole = router_ref[...]
     inv_norm = lax.rsqrt(jnp.sum(whole * whole, axis=0, keepdims=True) + EPS)
     low = (whole * inv_norm).astype(jnp.bfloat16)
@@ -96,7 +105,6 @@
         raised = jnp.exp(logits - jnp.max(logits, axis=1, keepdims=True))
         combine_ref[image] = raised / jnp.sum(raised, axis=1, keepdims=True)
     put_pair(sent_ref, 0, *slot_in)
-    fetch.wait()
     slot_grad = [
         contract_first(combine_ref[image].astype(jnp.bfloat16), out_grad_ref[image])
         for image in range(pictures)
@@ -140,18 +148,22 @@
         )
         hidden_ref[:, block] = activated.astype(jnp.bfloat16)
         slope_ref[:, block] = gelu_slope
-    write_out(hidden_ref, hidden_hbm)
+        write_out(hidden_ref.at[:, block], hidden_hbm.at[:, block])
     peers = recv_ref.shape[0]
     slot_out = jnp.dot(hidden_ref[...], w_out_ref[0], preferred_element_type=jnp.float32)
     put_pair(sent_ref, 0, slot_out[:peers], slot_out[peers:])
-    write_out(pair_rows(sent_ref, 0), pair_rows(sent_hbm, 0))
+    for copy in pair_copies(sent_ref, sent_hbm, 0, sems, len(copies)):
+        copy.start()
+        copies.append(copy)
     for block in blocks:
         hidden_grad = contract_last(grads_ref[...], w_out_ref[0, block, :])
         pre_grad_ref[:, block] = (hidden_grad * slope_ref[:, block]).astype(jnp.bfloat16)
-    write_out(pre_grad_ref, pre_grad_hbm)
+        write_out(pre_grad_ref.at[:, block], pre_grad_hbm.at[:, block])
     slot_dx = contract_last(pre_grad_ref[...], w_in_ref[0])
     put_pair(sent_ref, 1, slot_dx[:peers], slot_dx[peers:])
-    write_out(pair_rows(sent_ref, 1), pair_rows(sent_hbm, 1))
+    for copy in pair_copies(sent_ref, sent_hbm, 1, sems, len(copies)):
+        copy.start()
+        copies.append(copy)
     for copy in copies:
         copy.wait()
 
@@ -176,19 +188,20 @@
     sems,
 ):
     fetches = [
-        pltpu.make_async_copy(pair_rows(recv_hbm, pair), pair_rows(recv_ref, pair), sems.at[3 + pair])
-        for pair in range(2)
+        pair_copies(recv_hbm, recv_ref, pair, sems, 3 + pair * PAIR_CUTS) for pair in range(2)
     ]
-    fetches[1].start()
-    fetches[0].start()
+    for copy in fetches[1] + fetches[0]:
+        copy.start()
     peers, width = recv_ref.shape[0], slot_out_ref.shape[1]
-    fetches[1].wait()
+    for copy in fetches[1]:
+        copy.wait()
     take_pair(recv_ref, 1, slot_dx_ref)
     save_dx = pltpu.make_async_copy(slot_dx_ref, slot_dx_hbm, sems.at[0])
     save_dx.start()
-    fetches[0].wait()
+    for copy in fetches[0]:
+        copy.wait()
     take_pair(recv_ref, 0, slot_out_ref)
-    hat_turned = jnp.zeros((peers, width), jnp.float32)
+    logit_grads = []
     for image in range(images_ref.shape[0]):
         picked = slice(image * peers, (image + 1) * peers)
         combine, dispatch = combine_ref[image], dispatch_ref[image]
@@ -202,10 +215,11 @@
         )
         logit_grad = (LOGIT_SCALE * (grad_combine + grad_dispatch)).astype(jnp.bfloat16)
         logit_grad_ref[image] = logit_grad
-        hat_turned += contract_first(logit_grad, images_ref[image])
+        logit_grads.append(logit_grad)
     save_logit = pltpu.make_async_copy(logit_grad_ref, logit_grad_hbm, sems.at[1])
     save_logit.start()
-    hat_part = hat_turned.T
+    all_tokens = images_ref[...].reshape(-1, width)
+    hat_part = contract_first(jnp.concatenate(logit_grads, axis=0), all_tokens).T
     moment_part = jnp.sum(low_ref[...].astype(jnp.float32) * hat_part, axis=0, keepdims=True)
     inv_norm = norm_ref[...]
     term = (hat_part - router_ref[...] * inv_norm * moment_part) * inv_norm
@@ -244,7 +258,7 @@
     per_token = ((pictures, tokens, experts), f32)
     sent, router_low, inv_norm, dispatch, combine = pl.pallas_call(
         route_kernel,
-        in_specs=[in_vmem, in_vmem, in_hbm],
+        in_specs=[in_vmem] * 3,
         out_specs=[in_vmem] * 5,
         out_shape=[
             jax.ShapeDtypeStruct(*message),
@@ -253,10 +267,9 @@
             jax.ShapeDtypeStruct(*per_token),
             jax.ShapeDtypeStruct(*per_token),
         ],
-        scratch_shapes=[pltpu.VMEM(out_grad.shape, bf16), pltpu.SemaphoreType.DMA],
         compiler_params=params,
         name="route",
-    )(router_whole, images, pltpu.with_memory_space_constraint(out_grad, pltpu.HBM))
+    )(router_whole, images, out_grad)
 
     arrived = exchange(sent)
     outs = [message] + [((rows, width), bf16)] * 2 + [((rows, hidden_width), bf16)] * 2
@@ -268,7 +281,7 @@
         scratch_shapes=[pltpu.VMEM(*out) for out in outs]
         + [
             pltpu.VMEM((rows, hidden_width), f32),
-            pltpu.SemaphoreType.DMA((6,)),
+            pltpu.SemaphoreType.DMA((2 + 2 * PAIR_CUTS + 2 * (hidden_width // FF_BLOCK),)),
         ],
         compiler_params=params,
         name="expert",
@@ -284,7 +297,11 @@
         out_specs=[in_hbm] * 3,
         out_shape=[pltpu.HBM(*out) for out in outs],
         scratch_shapes=[pltpu.VMEM(*out) for out in outs]
-        + [pltpu.VMEM((rows, width), bf16), pltpu.VMEM(*message), pltpu.SemaphoreType.DMA((5,))],
+        + [
+            pltpu.VMEM((rows, width), bf16),
+            pltpu.VMEM(*message),
+            pltpu.SemaphoreType.DMA((3 + 2 * PAIR_CUTS,)),
+        ],
         compiler_params=params,
         name="logit",
     )(pltpu.with_memory_space_constraint(returned, pltpu.HBM), router_whole, inv_norm, router_low, images, out_grad, dispatch, combine)

time: 104 us -> 102 us (0.981)
  Pallas kernels: 13.5 us -> 12.4 us
where the time goes in v4:
time: 102 us
  blocking collectives  48.2 us (47%)
  waiting for transfers between devices  18.2 us (18%)
  Pallas kernels  12.4 us (12%)
  matrix products  12.2 us (12%)
  starting transfers between devices  8.85 us (9%)
    all_to_all x2, blocking collectives, exchange(): return lax.all_to_all(blocks, AXES, split_axis=0, concat_axis=0, tiled=True)  48.2 us
    all_to_all x2, waiting for transfers between devices, exchange(): return lax.all_to_all(blocks, AXES, split_axis=0, concat_axis=0, tiled=True)  18.2 us
    dot_general x2, matrix products, contract_first(): lax.dot_general(left_side, right_side, (((0,), (0,)), ((), ())), preferre...  9.45 us
    all_to_all x2, starting transfers between devices, exchange(): return lax.all_to_all(blocks, AXES, split_axis=0, concat_axis=0, tiled=True)  8.85 us
    pallas_call x1, Pallas kernels, per_device(): pl.pallas_call(expert_kernel, in_specs=[in_vmem] * 3, out_specs=[in_hbm]...  7.3 us
    pallas_call x1, Pallas kernels, per_device(): pl.pallas_call(logit_kernel, in_specs=[in_hbm] + [in_vmem] * 7, out_specs...  3.44 us
  transfers between devices with their start and end apart: 2, of which 2 were waited for; matrix products, arithmetic and copies ran while one was open for 12% of the time, Pallas kernels for 0%

profile of v4, /device:TPU:1, one launch (start us, length us, event | category | flops | bytes accessed | tf_op | source)
XLA Modules:
  0.0 102.2 jit_solution(6653076075509695416)
XLA Ops:
  0.6 0.0 copy-start.3
  0.6 0.0 copy-start.2
  0.7 0.0 copy-start.4
  0.7 0.8 copy-done.4
  1.5 0.0 copy-start.1
  1.5 0.0 copy-start
  1.5 25.1 %all_to_all.20 = f32[128,8,128]{2,1,0:T(8,128)S(1)} all-to-all(f32[128,8,128]{2,1,0:T(8,128)S(1)} %spread.1), channel_id=1, replica_groups=mesh['exp'=32,'rep'=4] {'exp','rep'}, dimensions={0} | all-to-all | bytes 1048576 | tf_op jit(solution)/shard_map/all_to_all | solution.py:38
  26.6 0.0 copy-done.3
  26.6 0.0 copy-done.2
  26.6 1.6 %route.1 = (bf16[128,32,128]{2,1,0:T(8,128)(2,1)S(1)}, bf16[1024,128]{1,0:T(8,128)(2,1)S(1)}, f32[1,128]{1,0:T(1,128)S(1)}, f32[2,256,128]{2,1,0:T(8,128)S(1)}, f32[2,256,128]{2,1,0:T(8,128)S(1)}) custom-call(f32[1024,128]{1,0:T(8,128)S(1)} %bitcast.16, bf16[2,256,1024]{2,1,0:T(8,128)(2,1)S(1)} %copy-done.2, bf16[2,256,1024]{2,1,0:T(8,128)(2,1)S(1)} %copy-done.3), custom_call_target="tpu_custom_call" | custom-call | tf_op jit(solution)/shard_map/route/pallas_call | solution.py:259
  28.3 23.1 %all_to_all.21.recv_ref = bf16[128,32,128]{2,1,0:T(8,128)(2,1)S(1)} all-to-all(bf16[128,32,128]{2,1,0:T(8,128)(2,1)S(1)} %get-tuple-element.18), channel_id=1, replica_groups=mesh['exp'=32,'rep'=4] {'exp','rep'}, dimensions={0} | all-to-all | bytes 2097152 | tf_op jit(solution)/shard_map/all_to_all | solution.py:38
  51.4 0.0 copy-done.1
  51.4 0.0 copy-done
  51.4 7.3 %expert.1 = (bf16[128,32,128]{2,1,0:T(8,128)(2,1)}, bf16[256,1024]{1,0:T(8,128)(2,1)}, bf16[256,1024]{1,0:T(8,128)(2,1)}, bf16[256,2560]{1,0:T(8,128)(2,1)}, bf16[256,2560]{1,0:T(8,128)(2,1)}) custom-call(bf16[128,32,128]{2,1,0:T(8,128)(2,1)S(1)} %all_to_all.21.recv_ref, bf16[1,1024,2560]{2,1,0:T(8,128)(2,1)S(1)} %copy-done, bf16[1,2560,1024]{2,1,0:T(8,128)(2,1)S(1)} %copy-done.1), custom_call_target="tpu_custom_call" | custom-call | tf_op jit(solution)/shard_map/expert/pallas_call | solution.py:276
  58.7 4.9 %all-to-all-start.2 = ((bf16[128,32,128]{2,1,0:T(8,128)(2,1)}), bf16[128,32,128]{2,1,0:T(8,128)(2,1)}, u32[]{:S(2)}, u32[]{:S(2)}) async-start(bf16[128,32,128]{2,1,0:T(8,128)(2,1)} %get-tuple-element.19), calls=%async_computation.2 | async-start | bytes 2097152 | tf_op jit(solution)/shard_map/all_to_all | solution.py:38
  63.6 0.0 copy-start.5
  63.6 0.0 copy-start.7
  63.6 5.5 %fusion = bf16[1,1024,2560]{2,1,0:T(8,128)(2,1)} fusion(bf16[256,1024]{1,0:T(8,128)(2,1)} %get-tuple-element.25, bf16[256,2560]{1,0:T(8,128)(2,1)} %get-tuple-element.26), kind=kOutput, calls=%fused_computation.2 | convolution fusion | flops 1344798720 | bytes 7077888 | tf_op jit(solution)/shard_map/dot_general | solution.py:32
  69.2 0.0 copy-done.5
  69.2 0.0 copy-done.7
  69.2 3.9 %fusion.1 = bf16[1,2560,1024]{2,1,0:T(8,128)(2,1)} fusion(bf16[256,2560]{1,0:T(8,128)(2,1)S(1)} %copy-done.5, bf16[256,1024]{1,0:T(8,128)(2,1)S(1)} %copy-done.7), kind=kOutput, calls=%fused_computation.3 | convolution fusion | flops 1344798720 | bytes 7077888 | tf_op jit(solution)/shard_map/dot_general | solution.py:32
  73.1 9.7 %all-to-all-done.2.recv_hbm = bf16[128,32,128]{2,1,0:T(8,128)(2,1)} async-done(((bf16[128,32,128]{2,1,0:T(8,128)(2,1)}), bf16[128,32,128]{2,1,0:T(8,128)(2,1)}, u32[]{:S(2)}, u32[]{:S(2)}) %all-to-all-start.2) | async-done | bytes 1048608 | tf_op jit(solution)/shard_map/all_to_all | solution.py:38
  82.8 3.4 %logit.1 = (bf16[1024,128]{1,0:T(8,128)(2,1)}, bf16[2,256,128]{2,1,0:T(8,128)(2,1)}, bf16[256,1024]{1,0:T(8,128)(2,1)}) custom-call(bf16[128,32,128]{2,1,0:T(8,128)(2,1)} %all-to-all-done.2.recv_hbm, f32[1024,128]{1,0:T(8,128)S(1)} %bitcast.17, f32[1,128]{1,0:T(1,128)S(1)} %get-tuple-element.20.norm_ref, bf16[1024,128]{1,0:T(8,128)(2,1)S(1)} %get-tuple-element.21.low_ref, ...), custom_call_target="tpu_custom_call" | custom-call | tf_op jit(solution)/shard_map/logit/pallas_call | solution.py:294
  86.3 0.0 copy-start.6
  86.3 3.9 %all-to-all-start.3 = ((bf16[128,8,128]{2,1,0:T(8,128)(2,1)}), bf16[128,8,128]{2,1,0:T(8,128)(2,1)S(1)}, u32[]{:S(2)}, u32[]{:S(2)}) async-start(bf16[128,8,128]{2,1,0:T(8,128)(2,1)} %bitcast.19), calls=%async_computation.3 | async-start | bytes 524288 | tf_op jit(solution)/shard_map/all_to_all | solution.py:38
  90.2 1.3 %fusion.2 = f32[2,256,1024]{2,1,0:T(8,128)S(1)} fusion(bf16[2,256,128]{2,1,0:T(8,128)(2,1)} %get-tuple-element.24, bf16[1024,128]{1,0:T(8,128)(2,1)S(1)} %get-tuple-element.21.low_ref), kind=kOutput, calls=%fused_computation.6 | convolution fusion | flops 134217728 | bytes 2490368 | tf_op jit(solution)/shard_map/bte,de->btd/dot_general | solution.py:317
  91.5 0.0 copy-done.6
  91.6 1.4 %add_convert_fusion = bf16[2,256,1024]{2,1,0:T(8,128)(2,1)} fusion(f32[2,256,1024]{2,1,0:T(8,128)S(1)} %fusion.2, bf16[2,128,1024]{2,1,0:T(8,128)(2,1)S(1)} %bitcast.18, f32[2,256,128]{2,1,0:T(8,128)S(1)} %get-tuple-element.17.dispatch_ref), kind=kOutput, calls=%fused_computation.4 | convolution fusion | flops 135331840 | bytes 3932160 | tf_op jit(solution)/shard_map/bte,bed->btd/dot_general | solution.py:311
  93.0 8.5 %all-to-all-done.3 = bf16[128,8,128]{2,1,0:T(8,128)(2,1)S(1)} async-done(((bf16[128,8,128]{2,1,0:T(8,128)(2,1)}), bf16[128,8,128]{2,1,0:T(8,128)(2,1)S(1)}, u32[]{:S(2)}, u32[]{:S(2)}) %all-to-all-start.3) | async-done | bytes 262176 | tf_op jit(solution)/shard_map/all_to_all | solution.py:38
  101.5 0.7 convert_reduce_fusion
  (1 shorter events, 0.0 us)
Async XLA Ops:
  0.6 26.0 %copy-start.3 = (bf16[2,256,1024]{2,1,0:T(8,128)(2,1)S(1)}, bf16[2,256,1024]{2,1,0:T(8,128)(2,1)}, u32[]{:S(2)}) copy-start(bf16[2,256,1024]{2,1,0:T(8,128)(2,1)} %out_grad_ref.3) | copy-start | bytes 3145732
  0.6 26.0 %copy-start.2 = (bf16[2,256,1024]{2,1,0:T(8,128)(2,1)S(1)}, bf16[2,256,1024]{2,1,0:T(8,128)(2,1)}, u32[]{:S(2)}) copy-start(bf16[2,256,1024]{2,1,0:T(8,128)(2,1)} %images_ref.3) | copy-start | bytes 3145732
  0.7 0.8 copy-start.4
  1.5 49.9 %copy-start.1 = (bf16[1,2560,1024]{2,1,0:T(8,128)(2,1)S(1)}, bf16[1,2560,1024]{2,1,0:T(8,128)(2,1)}, u32[]{:S(2)}) copy-start(bf16[1,2560,1024]{2,1,0:T(8,128)(2,1)} %w_out_ref.1) | copy-start | bytes 15728644
  1.5 49.9 %copy-start = (bf16[1,1024,2560]{2,1,0:T(8,128)(2,1)S(1)}, bf16[1,1024,2560]{2,1,0:T(8,128)(2,1)}, u32[]{:S(2)}) copy-start(bf16[1,1024,2560]{2,1,0:T(8,128)(2,1)} %w_in_ref.1) | copy-start | bytes 15728644
  58.7 24.1 %all-to-all-start.2 = ((bf16[128,32,128]{2,1,0:T(8,128)(2,1)}), bf16[128,32,128]{2,1,0:T(8,128)(2,1)}, u32[]{:S(2)}, u32[]{:S(2)}) async-start(bf16[128,32,128]{2,1,0:T(8,128)(2,1)} %get-tuple-element.19), calls=%async_computation.2 | async-start | bytes 2097152 | tf_op jit(solution)/shard_map/all_to_all | solution.py:38
  63.6 5.6 %copy-start.5 = (bf16[256,2560]{1,0:T(8,128)(2,1)S(1)}, bf16[256,2560]{1,0:T(8,128)(2,1)}, u32[]{:S(2)}) copy-start(bf16[256,2560]{1,0:T(8,128)(2,1)} %get-tuple-element.27) | copy-start | bytes 3932164
  63.6 5.5 %copy-start.7 = (bf16[256,1024]{1,0:T(8,128)(2,1)S(1)}, bf16[256,1024]{1,0:T(8,128)(2,1)}, u32[]{:S(2)}) copy-start(bf16[256,1024]{1,0:T(8,128)(2,1)} %get-tuple-element.28) | copy-start | bytes 1572868
  86.3 5.3 %copy-start.6 = (bf16[256,1024]{1,0:T(8,128)(2,1)S(1)}, bf16[256,1024]{1,0:T(8,128)(2,1)}, u32[]{:S(2)}) copy-start(bf16[256,1024]{1,0:T(8,128)(2,1)} %get-tuple-element.23) | copy-start | bytes 1572868
  86.3 15.2 %all-to-all-start.3 = ((bf16[128,8,128]{2,1,0:T(8,128)(2,1)}), bf16[128,8,128]{2,1,0:T(8,128)(2,1)S(1)}, u32[]{:S(2)}, u32[]{:S(2)}) async-start(bf16[128,8,128]{2,1,0:T(8,128)(2,1)} %bitcast.19), calls=%async_computation.3 | async-start | bytes 524288 | tf_op jit(solution)/shard_map/all_to_all | solution.py:38

commit v5 on v4

--- a/solution.py
+++ b/solution.py
@@ -11,7 +11,7 @@
 INV_ROOT = 0.3989422804014327
 AXES = ("exp", "rep")
 LANES = 128
-FF_BLOCK = 512
+FF_BLOCK = 1280
 PAIR_CUTS = 4
 VMEM_BYTES = 24 * 1024 * 1024
 

time: 102 us -> 102 us (level)
  no operation moved by 1% of the time
where the time goes in v5:
time: 102 us
  blocking collectives  48.2 us (47%)
  waiting for transfers between devices  18.2 us (18%)
  matrix products  12.2 us (12%)
  Pallas kernels  12.1 us (12%)
  starting transfers between devices  8.83 us (9%)
    all_to_all x2, blocking collectives, exchange(): return lax.all_to_all(blocks, AXES, split_axis=0, concat_axis=0, tiled=True)  48.2 us
    all_to_all x2, waiting for transfers between devices, exchange(): return lax.all_to_all(blocks, AXES, split_axis=0, concat_axis=0, tiled=True)  18.2 us
    dot_general x2, matrix products, contract_first(): lax.dot_general(left_side, right_side, (((0,), (0,)), ((), ())), preferre...  9.44 us
    all_to_all x2, starting transfers between devices, exchange(): return lax.all_to_all(blocks, AXES, split_axis=0, concat_axis=0, tiled=True)  8.83 us
    pallas_call x1, Pallas kernels, per_device(): pl.pallas_call(expert_kernel, in_specs=[in_vmem] * 3, out_specs=[in_hbm]...  7.02 us
    pallas_call x1, Pallas kernels, per_device(): pl.pallas_call(logit_kernel, in_specs=[in_hbm] + [in_vmem] * 7, out_specs...  3.44 us
  transfers between devices with their start and end apart: 2, of which 2 were waited for; matrix products, arithmetic and copies ran while one was open for 12% of the time, Pallas kernels for 0%

profile of v5, /device:TPU:1, one launch (start us, length us, event | category | flops | bytes accessed | tf_op | source)
XLA Modules:
  0.0 101.9 jit_solution(7158042094121342206)
XLA Ops:
  0.6 0.0 copy-start.3
  0.6 0.0 copy-start.2
  0.7 0.0 copy-start.4
  0.7 0.8 copy-done.4
  1.5 0.0 copy-start.1
  1.5 0.0 copy-start
  1.5 25.1 %all_to_all.20 = f32[128,8,128]{2,1,0:T(8,128)S(1)} all-to-all(f32[128,8,128]{2,1,0:T(8,128)S(1)} %spread.1), channel_id=1, replica_groups=mesh['exp'=32,'rep'=4] {'exp','rep'}, dimensions={0} | all-to-all | bytes 1048576 | tf_op jit(solution)/shard_map/all_to_all | solution.py:38
  26.6 0.0 copy-done.3
  26.6 0.0 copy-done.2
  26.6 1.6 %route.1 = (bf16[128,32,128]{2,1,0:T(8,128)(2,1)S(1)}, bf16[1024,128]{1,0:T(8,128)(2,1)S(1)}, f32[1,128]{1,0:T(1,128)S(1)}, f32[2,256,128]{2,1,0:T(8,128)S(1)}, f32[2,256,128]{2,1,0:T(8,128)S(1)}) custom-call(f32[1024,128]{1,0:T(8,128)S(1)} %bitcast.16, bf16[2,256,1024]{2,1,0:T(8,128)(2,1)S(1)} %copy-done.2, bf16[2,256,1024]{2,1,0:T(8,128)(2,1)S(1)} %copy-done.3), custom_call_target="tpu_custom_call" | custom-call | tf_op jit(solution)/shard_map/route/pallas_call | solution.py:259
  28.3 23.1 %all_to_all.21.recv_ref = bf16[128,32,128]{2,1,0:T(8,128)(2,1)S(1)} all-to-all(bf16[128,32,128]{2,1,0:T(8,128)(2,1)S(1)} %get-tuple-element.18), channel_id=1, replica_groups=mesh['exp'=32,'rep'=4] {'exp','rep'}, dimensions={0} | all-to-all | bytes 2097152 | tf_op jit(solution)/shard_map/all_to_all | solution.py:38
  51.4 0.0 copy-done.1
  51.4 0.0 copy-done
  51.4 7.0 %expert.1 = (bf16[128,32,128]{2,1,0:T(8,128)(2,1)}, bf16[256,1024]{1,0:T(8,128)(2,1)}, bf16[256,1024]{1,0:T(8,128)(2,1)}, bf16[256,2560]{1,0:T(8,128)(2,1)}, bf16[256,2560]{1,0:T(8,128)(2,1)}) custom-call(bf16[128,32,128]{2,1,0:T(8,128)(2,1)S(1)} %all_to_all.21.recv_ref, bf16[1,1024,2560]{2,1,0:T(8,128)(2,1)S(1)} %copy-done, bf16[1,2560,1024]{2,1,0:T(8,128)(2,1)S(1)} %copy-done.1), custom_call_target="tpu_custom_call" | custom-call | tf_op jit(solution)/shard_map/expert/pallas_call | solution.py:276
  58.4 4.9 %all-to-all-start.2 = ((bf16[128,32,128]{2,1,0:T(8,128)(2,1)}), bf16[128,32,128]{2,1,0:T(8,128)(2,1)}, u32[]{:S(2)}, u32[]{:S(2)}) async-start(bf16[128,32,128]{2,1,0:T(8,128)(2,1)} %get-tuple-element.19), calls=%async_computation.2 | async-start | bytes 2097152 | tf_op jit(solution)/shard_map/all_to_all | solution.py:38
  63.3 0.0 copy-start.5
  63.3 0.0 copy-start.7
  63.4 5.5 %fusion = bf16[1,1024,2560]{2,1,0:T(8,128)(2,1)} fusion(bf16[256,1024]{1,0:T(8,128)(2,1)} %get-tuple-element.25, bf16[256,2560]{1,0:T(8,128)(2,1)} %get-tuple-element.26), kind=kOutput, calls=%fused_computation.2 | convolution fusion | flops 1344798720 | bytes 7077888 | tf_op jit(solution)/shard_map/dot_general | solution.py:32
  68.9 0.0 copy-done.5
  68.9 0.0 copy-done.7
  68.9 3.9 %fusion.1 = bf16[1,2560,1024]{2,1,0:T(8,128)(2,1)} fusion(bf16[256,2560]{1,0:T(8,128)(2,1)S(1)} %copy-done.5, bf16[256,1024]{1,0:T(8,128)(2,1)S(1)} %copy-done.7), kind=kOutput, calls=%fused_computation.3 | convolution fusion | flops 1344798720 | bytes 7077888 | tf_op jit(solution)/shard_map/dot_general | solution.py:32
  72.8 9.7 %all-to-all-done.2.recv_hbm = bf16[128,32,128]{2,1,0:T(8,128)(2,1)} async-done(((bf16[128,32,128]{2,1,0:T(8,128)(2,1)}), bf16[128,32,128]{2,1,0:T(8,128)(2,1)}, u32[]{:S(2)}, u32[]{:S(2)}) %all-to-all-start.2) | async-done | bytes 1048608 | tf_op jit(solution)/shard_map/all_to_all | solution.py:38
  82.5 3.4 %logit.1 = (bf16[1024,128]{1,0:T(8,128)(2,1)}, bf16[2,256,128]{2,1,0:T(8,128)(2,1)}, bf16[256,1024]{1,0:T(8,128)(2,1)}) custom-call(bf16[128,32,128]{2,1,0:T(8,128)(2,1)} %all-to-all-done.2.recv_hbm, f32[1024,128]{1,0:T(8,128)S(1)} %bitcast.17, f32[1,128]{1,0:T(1,128)S(1)} %get-tuple-element.20.norm_ref, bf16[1024,128]{1,0:T(8,128)(2,1)S(1)} %get-tuple-element.21.low_ref, ...), custom_call_target="tpu_custom_call" | custom-call | tf_op jit(solution)/shard_map/logit/pallas_call | solution.py:294
  86.0 0.0 copy-start.6
  86.0 3.9 %all-to-all-start.3 = ((bf16[128,8,128]{2,1,0:T(8,128)(2,1)}), bf16[128,8,128]{2,1,0:T(8,128)(2,1)S(1)}, u32[]{:S(2)}, u32[]{:S(2)}) async-start(bf16[128,8,128]{2,1,0:T(8,128)(2,1)} %bitcast.19), calls=%async_computation.3 | async-start | bytes 524288 | tf_op jit(solution)/shard_map/all_to_all | solution.py:38
  89.9 1.3 %fusion.2 = f32[2,256,1024]{2,1,0:T(8,128)S(1)} fusion(bf16[2,256,128]{2,1,0:T(8,128)(2,1)} %get-tuple-element.24, bf16[1024,128]{1,0:T(8,128)(2,1)S(1)} %get-tuple-element.21.low_ref), kind=kOutput, calls=%fused_computation.6 | convolution fusion | flops 134217728 | bytes 2490368 | tf_op jit(solution)/shard_map/bte,de->btd/dot_general | solution.py:317
  91.3 0.0 copy-done.6
  91.3 1.4 %add_convert_fusion = bf16[2,256,1024]{2,1,0:T(8,128)(2,1)} fusion(f32[2,256,1024]{2,1,0:T(8,128)S(1)} %fusion.2, bf16[2,128,1024]{2,1,0:T(8,128)(2,1)S(1)} %bitcast.18, f32[2,256,128]{2,1,0:T(8,128)S(1)} %get-tuple-element.17.dispatch_ref), kind=kOutput, calls=%fused_computation.4 | convolution fusion | flops 135331840 | bytes 3932160 | tf_op jit(solution)/shard_map/bte,bed->btd/dot_general | solution.py:311
  92.7 8.5 %all-to-all-done.3 = bf16[128,8,128]{2,1,0:T(8,128)(2,1)S(1)} async-done(((bf16[128,8,128]{2,1,0:T(8,128)(2,1)}), bf16[128,8,128]{2,1,0:T(8,128)(2,1)S(1)}, u32[]{:S(2)}, u32[]{:S(2)}) %all-to-all-start.3) | async-done | bytes 262176 | tf_op jit(solution)/shard_map/all_to_all | solution.py:38
  101.2 0.7 convert_reduce_fusion
  (1 shorter events, 0.0 us)
Async XLA Ops:
  0.6 26.0 %copy-start.3 = (bf16[2,256,1024]{2,1,0:T(8,128)(2,1)S(1)}, bf16[2,256,1024]{2,1,0:T(8,128)(2,1)}, u32[]{:S(2)}) copy-start(bf16[2,256,1024]{2,1,0:T(8,128)(2,1)} %out_grad_ref.3) | copy-start | bytes 3145732
  0.6 26.0 %copy-start.2 = (bf16[2,256,1024]{2,1,0:T(8,128)(2,1)S(1)}, bf16[2,256,1024]{2,1,0:T(8,128)(2,1)}, u32[]{:S(2)}) copy-start(bf16[2,256,1024]{2,1,0:T(8,128)(2,1)} %images_ref.3) | copy-start | bytes 3145732
  0.7 0.8 copy-start.4
  1.5 49.9 %copy-start.1 = (bf16[1,2560,1024]{2,1,0:T(8,128)(2,1)S(1)}, bf16[1,2560,1024]{2,1,0:T(8,128)(2,1)}, u32[]{:S(2)}) copy-start(bf16[1,2560,1024]{2,1,0:T(8,128)(2,1)} %w_out_ref.1) | copy-start | bytes 15728644
  1.5 49.9 %copy-start = (bf16[1,1024,2560]{2,1,0:T(8,128)(2,1)S(1)}, bf16[1,1024,2560]{2,1,0:T(8,128)(2,1)}, u32[]{:S(2)}) copy-start(bf16[1,1024,2560]{2,1,0:T(8,128)(2,1)} %w_in_ref.1) | copy-start | bytes 15728644
  58.4 24.1 %all-to-all-start.2 = ((bf16[128,32,128]{2,1,0:T(8,128)(2,1)}), bf16[128,32,128]{2,1,0:T(8,128)(2,1)}, u32[]{:S(2)}, u32[]{:S(2)}) async-start(bf16[128,32,128]{2,1,0:T(8,128)(2,1)} %get-tuple-element.19), calls=%async_computation.2 | async-start | bytes 2097152 | tf_op jit(solution)/shard_map/all_to_all | solution.py:38
  63.3 5.6 %copy-start.5 = (bf16[256,2560]{1,0:T(8,128)(2,1)S(1)}, bf16[256,2560]{1,0:T(8,128)(2,1)}, u32[]{:S(2)}) copy-start(bf16[256,2560]{1,0:T(8,128)(2,1)} %get-tuple-element.27) | copy-start | bytes 3932164
  63.3 5.5 %copy-start.7 = (bf16[256,1024]{1,0:T(8,128)(2,1)S(1)}, bf16[256,1024]{1,0:T(8,128)(2,1)}, u32[]{:S(2)}) copy-start(bf16[256,1024]{1,0:T(8,128)(2,1)} %get-tuple-element.28) | copy-start | bytes 1572868
  86.0 5.3 %copy-start.6 = (bf16[256,1024]{1,0:T(8,128)(2,1)S(1)}, bf16[256,1024]{1,0:T(8,128)(2,1)}, u32[]{:S(2)}) copy-start(bf16[256,1024]{1,0:T(8,128)(2,1)} %get-tuple-element.23) | copy-start | bytes 1572868
  86.0 15.2 %all-to-all-start.3 = ((bf16[128,8,128]{2,1,0:T(8,128)(2,1)}), bf16[128,8,128]{2,1,0:T(8,128)(2,1)S(1)}, u32[]{:S(2)}, u32[]{:S(2)}) async-start(bf16[128,8,128]{2,1,0:T(8,128)(2,1)} %bitcast.19), calls=%async_computation.3 | async-start | bytes 524288 | tf_op jit(solution)/shard_map/all_to_all | solution.py:38

commit v6 on v5

--- a/solution.py
+++ b/solution.py
@@ -3,13 +3,15 @@
 from jax import lax
 from jax.experimental import pallas as pl
 from jax.experimental.pallas import tpu as pltpu
+from jax.sharding import Mesh
 from jax.sharding import PartitionSpec as P
 
 LOGIT_SCALE = 2.0
 EPS = 1e-06
 SQRT_HALF = 0.7071067811865476
 INV_ROOT = 0.3989422804014327
-AXES = ("exp", "rep")
+CORES = 2
+AXES = ("chip", "core", "rep")
 LANES = 128
 FF_BLOCK = 1280
 PAIR_CUTS = 4
@@ -34,8 +36,8 @@
     )
 
 
-def exchange(blocks):
-    return lax.all_to_all(blocks, AXES, split_axis=0, concat_axis=0, tiled=True)
+def exchange(blocks, axes=AXES):
+    return lax.all_to_all(blocks, axes, split_axis=0, concat_axis=0, tiled=True)
 
 
 def put_pair(messages_ref, pair, first, second):
@@ -79,16 +81,22 @@
 
 
 def route_kernel(
-    router_ref,
+    own_ref,
+    other_ref,
     images_ref,
     out_grad_ref,
     sent_ref,
+    router_ref,
     low_ref,
     norm_ref,
     dispatch_ref,
     combine_ref,
 ):
-    whole = router_ref[...]
+    on_first = lax.axis_index("core") == 0
+    own, other = own_ref[...], other_ref[...]
+    halves = [jnp.where(on_first, own, other), jnp.where(on_first, other, own)]
+    whole = jnp.stack(halves, axis=1).reshape(router_ref.shape)
+    router_ref[...] = whole
     inv_norm = lax.rsqrt(jnp.sum(whole * whole, axis=0, keepdims=True) + EPS)
     low = (whole * inv_norm).astype(jnp.bfloat16)
     low_ref[...] = low
@@ -246,22 +254,27 @@
         spread_kernel,
         in_specs=[in_vmem],
         out_specs=in_vmem,
-        out_shape=jax.ShapeDtypeStruct((devices, own_rows, experts), f32),
+        out_shape=jax.ShapeDtypeStruct((devices // CORES, own_rows, experts), f32),
         compiler_params=params,
         cost_estimate=pl.CostEstimate(
             flops=20_000_000_000, bytes_accessed=30_000_000, transcendentals=300_000
         ),
         name="spread",
     )(router)
-    router_whole = exchange(copies).reshape(width, experts)
+    own_half = exchange(copies, ("chip", "rep"))
+    own_half = own_half.reshape(lax.axis_size("chip"), -1, experts)
+    other_half = lax.ppermute(
+        own_half, "core", [(core, CORES - 1 - core) for core in range(CORES)]
+    )
     message = ((devices, 4 * width // LANES, LANES), bf16)
     per_token = ((pictures, tokens, experts), f32)
-    sent, router_low, inv_norm, dispatch, combine = pl.pallas_call(
+    sent, router_whole, router_low, inv_norm, dispatch, combine = pl.pallas_call(
         route_kernel,
-        in_specs=[in_vmem] * 3,
-        out_specs=[in_vmem] * 5,
+        in_specs=[in_vmem] * 4,
+        out_specs=[in_vmem] * 6,
         out_shape=[
             jax.ShapeDtypeStruct(*message),
+            jax.ShapeDtypeStruct((width, experts), f32),
             jax.ShapeDtypeStruct((width, experts), bf16),
             jax.ShapeDtypeStruct((1, experts), f32),
             jax.ShapeDtypeStruct(*per_token),
@@ -269,7 +282,7 @@
         ],
         compiler_params=params,
         name="route",
-    )(router_whole, images, out_grad)
+    )(own_half, other_half, images, out_grad)
 
     arrived = exchange(sent)
     outs = [message] + [((rows, width), bf16)] * 2 + [((rows, hidden_width), bf16)] * 2
@@ -320,6 +333,9 @@
 
 
 def solution(mesh):
+    devices = mesh.devices
+    pairs = (devices.shape[0] // CORES, CORES, devices.shape[1])
+    mesh = Mesh(devices.reshape(pairs), AXES)
     in_specs = (
         P(AXES, None, None),
         P(AXES, None),

time: 102 us -> 102 us (level)
  blocking collectives: 48.2 us -> 44.5 us
  starting transfers between devices: 8.83 us -> 10.9 us
  waiting for transfers between devices: 18.2 us -> 19.4 us
    all_to_all x2, blocking collectives: 48.2 us -> 44.5 us  [exchange(): return lax.all_to_all(blocks, axes, split_axis=0, concat_axis=0, tiled=True)]
    ppermute x0 -> x1, starting transfers between devices: none -> 2.09 us  [per_device(): lax.ppermute(own_half, 'core', [(core, CORES - 1 - core) for core in rang...]
    ppermute x0 -> x1, waiting for transfers between devices: none -> 1.16 us  [per_device(): lax.ppermute(own_half, 'core', [(core, CORES - 1 - core) for core in rang...]
  transfers between devices with their start and end apart: 2 -> 3, of which waited for: 2 -> 3; matrix products, arithmetic and copies ran while one was open for 12% -> 12% of each run, Pallas kernels for 0% -> 0%
where the time goes in v6:
time: 102 us
  blocking collectives  44.5 us (44%)
  waiting for transfers between devices  19.4 us (19%)
  Pallas kernels  12.6 us (12%)
  matrix products  12.2 us (12%)
  starting transfers between devices  10.9 us (11%)
    all_to_all x2, blocking collectives, exchange(): return lax.all_to_all(blocks, axes, split_axis=0, concat_axis=0, tiled=True)  44.5 us
    all_to_all x2, waiting for transfers between devices, exchange(): return lax.all_to_all(blocks, axes, split_axis=0, concat_axis=0, tiled=True)  18.2 us
    dot_general x2, matrix products, contract_first(): lax.dot_general(left_side, right_side, (((0,), (0,)), ((), ())), preferre...  9.44 us
    all_to_all x2, starting transfers between devices, exchange(): return lax.all_to_all(blocks, axes, split_axis=0, concat_axis=0, tiled=True)  8.83 us
    pallas_call x1, Pallas kernels, per_device(): pl.pallas_call(expert_kernel, in_specs=[in_vmem] * 3, out_specs=[in_hbm]...  7.39 us
    pallas_call x1, Pallas kernels, per_device(): pl.pallas_call(logit_kernel, in_specs=[in_hbm] + [in_vmem] * 7, out_specs...  3.43 us
    ppermute x1, starting transfers between devices, per_device(): lax.ppermute(own_half, 'core', [(core, CORES - 1 - core) for core in rang...  2.09 us
  transfers between devices with their start and end apart: 3, of which 3 were waited for; matrix products, arithmetic and copies ran while one was open for 12% of the time, Pallas kernels for 0%

profile of v6, /device:TPU:1, one launch (start us, length us, event | category | flops | bytes accessed | tf_op | source)
XLA Modules:
  0.0 101.9 jit_solution(2735090326638884434)
XLA Ops:
  0.6 0.0 copy-start.3
  0.6 0.0 copy-start.2
  0.7 0.0 copy-start.4
  0.7 0.8 copy-done.4
  1.5 0.0 copy-start.1
  1.5 0.0 copy-start
  1.5 21.5 %all_to_all.20 = f32[64,8,128]{2,1,0:T(8,128)S(1)} all-to-all(f32[64,8,128]{2,1,0:T(8,128)S(1)} %spread.1), channel_id=1, replica_groups=mesh['chip'=16,'core'=2,'rep'=4] {'chip','rep'}, dimensions={0} | all-to-all | bytes 524288 | tf_op jit(solution)/shard_map/all_to_all | solution.py:40
  23.0 2.1 %collective-permute-start = (f32[16,32,128]{2,1,0:T(8,128)S(1)}, f32[16,32,128]{2,1,0:T(8,128)S(1)}, u32[]{:S(2)}, u32[]{:S(2)}) collective-permute-start(f32[16,32,128]{2,1,0:T(8,128)S(1)} %bitcast.16), channel_id=1, source_target_pairs={{0,4},{4,0},{1,5},{5,1},{2,6},{6,2},{3,7},{7,3},{8,12},{12,8},{9,1... | collective-permute-start | bytes 786440 | tf_op jit(solution)/shard_map/ppermute | solution.py:266
  25.1 1.2 %collective-permute-done.other_ref = f32[16,32,128]{2,1,0:T(8,128)S(1)} collective-permute-done((f32[16,32,128]{2,1,0:T(8,128)S(1)}, f32[16,32,128]{2,1,0:T(8,128)S(1)}, u32[]{:S(2)}, u32[]{:S(2)}) %collective-permute-start) | collective-permute-done | bytes 262176 | tf_op jit(solution)/shard_map/ppermute | solution.py:266
  26.2 0.0 copy-done.3
  26.2 0.0 copy-done.2
  26.2 1.7 %route.1 = (bf16[128,32,128]{2,1,0:T(8,128)(2,1)S(1)}, f32[1024,128]{1,0:T(8,128)S(1)}, bf16[1024,128]{1,0:T(8,128)(2,1)S(1)}, f32[1,128]{1,0:T(1,128)S(1)}, f32...) custom-call(f32[16,32,128]{2,1,0:T(8,128)S(1)} %bitcast.17, f32[16,32,128]{2,1,0:T(8,128)S(1)} %collective-permute-done.other_ref, ...), custom_call_target="tpu_custom_call" | custom-call | tf_op jit(solution)/shard_map/route/pallas_call | solution.py:271
  28.0 23.1 %all_to_all.21.recv_ref = bf16[128,32,128]{2,1,0:T(8,128)(2,1)S(1)} all-to-all(bf16[128,32,128]{2,1,0:T(8,128)(2,1)S(1)} %get-tuple-element.19), channel_id=1, replica_groups=mesh['chip'=16,'core'=2,'rep'=4] {'chip','core','rep'}, dimensions={0} | all-to-all | bytes 2097152 | tf_op jit(solution)/shard_map/all_to_all | solution.py:40
  51.0 0.0 copy-done.1
  51.0 0.0 copy-done
  51.0 7.4 %expert.1 = (bf16[128,32,128]{2,1,0:T(8,128)(2,1)}, bf16[256,1024]{1,0:T(8,128)(2,1)}, bf16[256,1024]{1,0:T(8,128)(2,1)}, bf16[256,2560]{1,0:T(8,128)(2,1)}, bf16[256,2560]{1,0:T(8,128)(2,1)}) custom-call(bf16[128,32,128]{2,1,0:T(8,128)(2,1)S(1)} %all_to_all.21.recv_ref, bf16[1,1024,2560]{2,1,0:T(8,128)(2,1)S(1)} %copy-done, bf16[1,2560,1024]{2,1,0:T(8,128)(2,1)S(1)} %copy-done.1), custom_call_target="tpu_custom_call" | custom-call | tf_op jit(solution)/shard_map/expert/pallas_call | solution.py:289
  58.4 4.9 %all-to-all-start.2 = ((bf16[128,32,128]{2,1,0:T(8,128)(2,1)}), bf16[128,32,128]{2,1,0:T(8,128)(2,1)}, u32[]{:S(2)}, u32[]{:S(2)}) async-start(bf16[128,32,128]{2,1,0:T(8,128)(2,1)} %get-tuple-element.20), calls=%async_computation.2 | async-start | bytes 2097152 | tf_op jit(solution)/shard_map/all_to_all | solution.py:40
  63.4 0.0 copy-start.5
  63.4 0.0 copy-start.7
  63.4 5.5 %fusion = bf16[1,1024,2560]{2,1,0:T(8,128)(2,1)} fusion(bf16[256,1024]{1,0:T(8,128)(2,1)} %get-tuple-element.27, bf16[256,2560]{1,0:T(8,128)(2,1)} %get-tuple-element.28), kind=kOutput, calls=%fused_computation.2 | convolution fusion | flops 1344798720 | bytes 7077888 | tf_op jit(solution)/shard_map/dot_general | solution.py:34
  68.9 0.0 copy-done.5
  68.9 0.0 copy-done.7
  68.9 3.9 %fusion.1 = bf16[1,2560,1024]{2,1,0:T(8,128)(2,1)} fusion(bf16[256,2560]{1,0:T(8,128)(2,1)S(1)} %copy-done.5, bf16[256,1024]{1,0:T(8,128)(2,1)S(1)} %copy-done.7), kind=kOutput, calls=%fused_computation.3 | convolution fusion | flops 1344798720 | bytes 7077888 | tf_op jit(solution)/shard_map/dot_general | solution.py:34
  72.8 9.7 %all-to-all-done.2.recv_hbm = bf16[128,32,128]{2,1,0:T(8,128)(2,1)} async-done(((bf16[128,32,128]{2,1,0:T(8,128)(2,1)}), bf16[128,32,128]{2,1,0:T(8,128)(2,1)}, u32[]{:S(2)}, u32[]{:S(2)}) %all-to-all-start.2) | async-done | bytes 1048608 | tf_op jit(solution)/shard_map/all_to_all | solution.py:40
  82.5 3.4 %logit.1 = (bf16[1024,128]{1,0:T(8,128)(2,1)}, bf16[2,256,128]{2,1,0:T(8,128)(2,1)}, bf16[256,1024]{1,0:T(8,128)(2,1)}) custom-call(bf16[128,32,128]{2,1,0:T(8,128)(2,1)} %all-to-all-done.2.recv_hbm, f32[1024,128]{1,0:T(8,128)S(1)} %get-tuple-element.21.router_ref, f32[1,128]{1,0:T(1,128)S(1)} %get-tuple-element.22.norm_ref, ...), custom_call_target="tpu_custom_call" | custom-call | tf_op jit(solution)/shard_map/logit/pallas_call | solution.py:307
  86.0 0.0 copy-start.6
  86.0 3.9 %all-to-all-start.3 = ((bf16[128,8,128]{2,1,0:T(8,128)(2,1)}), bf16[128,8,128]{2,1,0:T(8,128)(2,1)S(1)}, u32[]{:S(2)}, u32[]{:S(2)}) async-start(bf16[128,8,128]{2,1,0:T(8,128)(2,1)} %bitcast.19), calls=%async_computation.3 | async-start | bytes 524288 | tf_op jit(solution)/shard_map/all_to_all | solution.py:40
  89.9 1.3 %fusion.2 = f32[2,256,1024]{2,1,0:T(8,128)S(1)} fusion(bf16[2,256,128]{2,1,0:T(8,128)(2,1)} %get-tuple-element.26, bf16[1024,128]{1,0:T(8,128)(2,1)S(1)} %get-tuple-element.23.low_ref), kind=kOutput, calls=%fused_computation.6 | convolution fusion | flops 134217728 | bytes 2490368 | tf_op jit(solution)/shard_map/bte,de->btd/dot_general | solution.py:330
  91.3 0.0 copy-done.6
  91.3 1.4 %add_convert_fusion = bf16[2,256,1024]{2,1,0:T(8,128)(2,1)} fusion(f32[2,256,1024]{2,1,0:T(8,128)S(1)} %fusion.2, bf16[2,128,1024]{2,1,0:T(8,128)(2,1)S(1)} %bitcast.18, f32[2,256,128]{2,1,0:T(8,128)S(1)} %get-tuple-element.18.dispatch_ref), kind=kOutput, calls=%fused_computation.4 | convolution fusion | flops 135331840 | bytes 3932160 | tf_op jit(solution)/shard_map/bte,bed->btd/dot_general | solution.py:324
  92.7 8.5 %all-to-all-done.3 = bf16[128,8,128]{2,1,0:T(8,128)(2,1)S(1)} async-done(((bf16[128,8,128]{2,1,0:T(8,128)(2,1)}), bf16[128,8,128]{2,1,0:T(8,128)(2,1)S(1)}, u32[]{:S(2)}, u32[]{:S(2)}) %all-to-all-start.3) | async-done | bytes 262176 | tf_op jit(solution)/shard_map/all_to_all | solution.py:40
  101.2 0.7 convert_reduce_fusion
  (1 shorter events, 0.0 us)
Async XLA Ops:
  0.6 25.6 %copy-start.3 = (bf16[2,256,1024]{2,1,0:T(8,128)(2,1)S(1)}, bf16[2,256,1024]{2,1,0:T(8,128)(2,1)}, u32[]{:S(2)}) copy-start(bf16[2,256,1024]{2,1,0:T(8,128)(2,1)} %out_grad_ref.3) | copy-start | bytes 3145732
  0.6 25.6 %copy-start.2 = (bf16[2,256,1024]{2,1,0:T(8,128)(2,1)S(1)}, bf16[2,256,1024]{2,1,0:T(8,128)(2,1)}, u32[]{:S(2)}) copy-start(bf16[2,256,1024]{2,1,0:T(8,128)(2,1)} %images_ref.3) | copy-start | bytes 3145732
  0.7 0.8 copy-start.4
  1.5 49.6 %copy-start.1 = (bf16[1,2560,1024]{2,1,0:T(8,128)(2,1)S(1)}, bf16[1,2560,1024]{2,1,0:T(8,128)(2,1)}, u32[]{:S(2)}) copy-start(bf16[1,2560,1024]{2,1,0:T(8,128)(2,1)} %w_out_ref.1) | copy-start | bytes 15728644
  1.5 49.5 %copy-start = (bf16[1,1024,2560]{2,1,0:T(8,128)(2,1)S(1)}, bf16[1,1024,2560]{2,1,0:T(8,128)(2,1)}, u32[]{:S(2)}) copy-start(bf16[1,1024,2560]{2,1,0:T(8,128)(2,1)} %w_in_ref.1) | copy-start | bytes 15728644
  23.0 3.3 %collective-permute-start = (f32[16,32,128]{2,1,0:T(8,128)S(1)}, f32[16,32,128]{2,1,0:T(8,128)S(1)}, u32[]{:S(2)}, u32[]{:S(2)}) collective-permute-start(f32[16,32,128]{2,1,0:T(8,128)S(1)} %bitcast.16), channel_id=1, source_target_pairs={{0,4},{4,0},{1,5},{5,1},{2,6},{6,2},{3,7},{7,3},{8,12},{12,8},{9,1... | collective-permute-start | bytes 786440 | tf_op jit(solution)/shard_map/ppermute | solution.py:266
  58.4 24.1 %all-to-all-start.2 = ((bf16[128,32,128]{2,1,0:T(8,128)(2,1)}), bf16[128,32,128]{2,1,0:T(8,128)(2,1)}, u32[]{:S(2)}, u32[]{:S(2)}) async-start(bf16[128,32,128]{2,1,0:T(8,128)(2,1)} %get-tuple-element.20), calls=%async_computation.2 | async-start | bytes 2097152 | tf_op jit(solution)/shard_map/all_to_all | solution.py:40
  63.4 5.6 %copy-start.5 = (bf16[256,2560]{1,0:T(8,128)(2,1)S(1)}, bf16[256,2560]{1,0:T(8,128)(2,1)}, u32[]{:S(2)}) copy-start(bf16[256,2560]{1,0:T(8,128)(2,1)} %get-tuple-element.29) | copy-start | bytes 3932164
  63.4 5.5 %copy-start.7 = (bf16[256,1024]{1,0:T(8,128)(2,1)S(1)}, bf16[256,1024]{1,0:T(8,128)(2,1)}, u32[]{:S(2)}) copy-start(bf16[256,1024]{1,0:T(8,128)(2,1)} %get-tuple-element.30) | copy-start | bytes 1572868
  86.0 5.3 %copy-start.6 = (bf16[256,1024]{1,0:T(8,128)(2,1)S(1)}, bf16[256,1024]{1,0:T(8,128)(2,1)}, u32[]{:S(2)}) copy-start(bf16[256,1024]{1,0:T(8,128)(2,1)} %get-tuple-element.25) | copy-start | bytes 1572868
  86.0 15.2 %all-to-all-start.3 = ((bf16[128,8,128]{2,1,0:T(8,128)(2,1)}), bf16[128,8,128]{2,1,0:T(8,128)(2,1)S(1)}, u32[]{:S(2)}, u32[]{:S(2)}) async-start(bf16[128,8,128]{2,1,0:T(8,128)(2,1)} %bitcast.19), calls=%async_computation.3 | async-start | bytes 524288 | tf_op jit(solution)/shard_map/all_to_all | solution.py:40
